TPU v7x, 32 devices: a whole 2x2x4 slice. The times are simulated.
32 devices in a mesh: dp: 8 (over z, y), mp: 4 (over x, core).
Axes of the slice: x: 2, y: 2, z: 4, core: 2. Of those that a mesh axis runs over, the one named last changes fastest.
Arguments:
- token_ids: int32 [64, 512], P('dp'), may hold values from 0 to 30719
- segment_ids: int32 [64, 512], P('dp'), may hold values from 0 to 1, as said below
- task_ids: int32 [64], P('dp'), may hold values from 0 to 3, as said below
- task_order: int32 [4], replicated, may hold values from 0 to 3, each once
- counted: int32 [64, 512], P('dp'), may hold values from 0 to 1, as said below
- targets: float32 [64, 512], P('dp'), may hold values from -6 to 6
- word_table: float32 [15360, 1536], P('dp', 'mp'), may hold values from -0.24 to 0.24
- word_first: float32 [15360, 1536], P('dp', 'mp'), may hold values from -5.722046e-06 to 5.722046e-06
- word_second: float32 [15360, 1536], P('dp', 'mp'), may hold values from 8.043907e-14 to 3.217563e-13
- tables: float32 [514, 768], P(None, 'dp'), may hold values from -0.24 to 0.24
- tables_first: float32 [514, 768], P(None, 'dp'), may hold values from -5.722046e-06 to 5.722046e-06
- tables_second: float32 [514, 768], P(None, 'dp'), may hold values from 8.043907e-14 to 3.217563e-13
- matrices: float32 [768, 9216], P('dp', 'mp')
- matrices_first: float32 [768, 9216], P('dp', 'mp'), may hold values from -5.722046e-06 to 5.722046e-06
- matrices_second: float32 [768, 9216], P('dp', 'mp'), may hold values from 8.043907e-14 to 3.217563e-13
- vectors: float32 [14, 768], P(None, 'dp')
- vectors_first: float32 [14, 768], P(None, 'dp'), may hold values from -5.722046e-06 to 5.722046e-06
- vectors_second: float32 [14, 768], P(None, 'dp'), may hold values from 8.043907e-14 to 3.217563e-13
- regressor: float32 [4, 768], P(None, 'dp'), may hold values from -0.21875 to 0.21875
- regressor_first: float32 [4, 768], P(None, 'dp'), may hold values from -5.722046e-06 to 5.722046e-06
- regressor_second: float32 [4, 768], P(None, 'dp'), may hold values from 8.043907e-14 to 3.217563e-13
Outputs:
- word_grad: float32 [15360, 1536], P('dp', 'mp')
- word_moment: float32 [15360, 1536], P('dp', 'mp')
- word_square: float32 [15360, 1536], P('dp', 'mp')
- word_weight: float32 [15360, 1536], P('dp', 'mp')
- tables_grad: float32 [514, 768], P(None, 'dp')
- tables_moment: float32 [514, 768], P(None, 'dp')
- tables_square: float32 [514, 768], P(None, 'dp')
- tables_weight: float32 [514, 768], P(None, 'dp')
- matrices_grad: float32 [768, 9216], P('dp', 'mp')
- matrices_moment: float32 [768, 9216], P('dp', 'mp')
- matrices_square: float32 [768, 9216], P('dp', 'mp')
- matrices_weight: float32 [768, 9216], P('dp', 'mp')
- vectors_grad: float32 [14, 768], P(None, 'dp')
- vectors_moment: float32 [14, 768], P(None, 'dp')
- vectors_square: float32 [14, 768], P(None, 'dp')
- vectors_weight: float32 [14, 768], P(None, 'dp')
- regressor_grad: float32 [4, 768], P(None, 'dp')
- regressor_moment: float32 [4, 768], P(None, 'dp')
- regressor_square: float32 [4, 768], P(None, 'dp')
- regressor_weight: float32 [4, 768], P(None, 'dp')
- grad_norm: float32 [], replicated
- loss_total: float32 [], replicated
- task_counts: float32 [4], replicated
Inputs may be any that keep to these rules, and one draw needn't show every extreme that they name: `segment_ids`: each row holds zeros and then ones, both present; the first one stands between positions 128 and 384. `task_ids`: every task occurs in some example. `task_order`: A permutation of the 4 tasks. `counted`: position 0 of every example counts.
All inputs are finite; a program needn't handle non-finite values.
Results may differ from a plain program's by a relative error of at most 0.0035.
The roundings to bfloat16 on the way count: a program that leaves them out, or rounds other values in their place, can miss the bound.
Values may be sent and summed in bfloat16 or wider, within the bound.
No kernel may reach another device: no remote copies, remote signals or barrier semaphores. Data moves between devices by JAX's collectives and lax.ppermute only.
A program may use at most 384 MiB of HBM per device.

v0:
```python
import jax
import jax.numpy as jnp
from jax import lax
from jax.sharding import PartitionSpec as P

HEAD = 64
STEP = 5


HIGHEST = lax.Precision.HIGHEST
FLOAT = jnp.float32
BFLOAT = jnp.bfloat16
NORM_EPS = 1e-12
CLIP = 0.05
BETA_ONE = 0.9
BETA_TWO = 0.999
ADAM_EPS = 1e-08
RATE_WEIGHT = 0.03
RATE_VECTOR = 0.3
DECAY = 0.01


def layer_norm(inputs, norm_gain, norm_bias):
    center = jnp.mean(inputs, axis=-1, keepdims=True)
    offset = inputs - center
    spread = jnp.mean(offset * offset, axis=-1, keepdims=True)
    return offset * lax.rsqrt(spread + NORM_EPS) * norm_gain + norm_bias


def gelu_exact(inputs):
    return jax.nn.gelu(inputs, approximate=False)


def mixed_sum(partial_value):
    return lax.psum(partial_value, "mp")


def mixed_back(partial_value):
    return lax.psum(partial_value, "mp")


def split_heads(projected, slot_index):
    return projected[:, :, slot_index].reshape(
        projected.shape[0], projected.shape[1], projected.shape[3] // HEAD, HEAD
    )


def attention_scores(query_rows, key_rows):
    return jnp.einsum(
        "bqhe,bkhe->bhqk", query_rows, key_rows, preferred_element_type=FLOAT
    ) * HEAD ** (-0.5)


def layer_forward(hidden_zero, matrices, vector_full, vector_own):
    inputs_low = hidden_zero.astype(BFLOAT)
    projected = jnp.einsum(
        "bsd,dce->bsce", inputs_low, matrices[:, 0:3, :], preferred_element_type=FLOAT
    )
    biases = jnp.stack([vector_own[2], jnp.zeros_like(vector_own[2]), vector_own[3]])
    projected_low = (projected + biases).astype(BFLOAT)
    scores = attention_scores(split_heads(projected_low, 0), split_heads(projected_low, 1))
    log_total = jax.nn.logsumexp(scores, axis=-1, keepdims=True)
    weights = jnp.exp(scores - log_total).astype(BFLOAT)
    context = jnp.einsum(
        "bhqk,bkhe->bqhe", weights, split_heads(projected_low, 2), preferred_element_type=FLOAT
    )
    context = context.reshape(hidden_zero.shape[0], hidden_zero.shape[1], -1).astype(BFLOAT)
    attended = (
        mixed_sum(
            jnp.einsum("bsh,oh->bso", context, matrices[:, 3, :], preferred_element_type=FLOAT)
        )
        + vector_full[4]
    )
    residual_one = hidden_zero + attended
    hidden_one = layer_norm(residual_one, vector_full[5], vector_full[6])
    hidden_low = hidden_one.astype(BFLOAT)
    inner_sum = (
        jnp.einsum("bsd,dce->bsce", hidden_low, matrices[:, 4:8, :], preferred_element_type=FLOAT)
        + vector_own[7:11]
    )
    active = gelu_exact(inner_sum).astype(BFLOAT)
    branch_out = (
        mixed_sum(
            jnp.einsum("bsce,oce->bso", active, matrices[:, 8:12, :], preferred_element_type=FLOAT)
        )
        + vector_full[11]
    )
    residual_two = hidden_one + branch_out
    hidden_two = layer_norm(residual_two, vector_full[12], vector_full[13])
    saved_values = (
        inputs_low,
        projected_low,
        log_total,
        context,
        residual_one,
        hidden_low,
        inner_sum,
        active,
        residual_two,
    )
    return (hidden_two, saved_values)


def layer_backward(grad_output, matrices, vector_full, saved_values, column_start, task_low):
    (
        inputs_low,
        projected_low,
        log_total,
        context,
        residual_one,
        hidden_low,
        inner_sum,
        active,
        residual_two,
    ) = saved_values
    width_own = matrices.shape[2]
    norm_two = jax.vjp(layer_norm, residual_two, vector_full[12], vector_full[13])[1]
    grad_residual_two, gain_two, bias_two = norm_two(grad_output)
    grad_branch = grad_residual_two.astype(BFLOAT)
    grad_active = jnp.einsum(
        "bso,oce->bsce", grad_branch, matrices[:, 8:12, :], preferred_element_type=FLOAT
    )
    down_grad = jnp.einsum(
        "bso,bt,bsce->otce", grad_branch, task_low, active, preferred_element_type=FLOAT
    )
    grad_inner = jax.vjp(gelu_exact, inner_sum)[1](grad_active)[0].astype(BFLOAT)
    up_grad = jnp.einsum(
        "bsd,bt,bsce->dtce", hidden_low, task_low, grad_inner, preferred_element_type=FLOAT
    )
    grad_hidden_one = grad_residual_two + mixed_back(
        jnp.einsum("bsce,dce->bsd", grad_inner, matrices[:, 4:8, :], preferred_element_type=FLOAT)
    )
    norm_one = jax.vjp(layer_norm, residual_one, vector_full[5], vector_full[6])[1]
    grad_residual_one, gain_one, bias_one = norm_one(grad_hidden_one)
    grad_attended = grad_residual_one.astype(BFLOAT)
    grad_context = jnp.einsum(
        "bso,oh->bsh", grad_attended, matrices[:, 3, :], preferred_element_type=FLOAT
    ).astype(BFLOAT)
    output_grad = jnp.einsum(
        "bso,bt,bsh->oth", grad_attended, task_low, context, preferred_element_type=FLOAT
    )
    query_rows = split_heads(projected_low, 0)
    key_rows = split_heads(projected_low, 1)
    value_rows = split_heads(projected_low, 2)
    weights = jnp.exp(attention_scores(query_rows, key_rows) - log_total)
    grad_heads = grad_context.reshape(query_rows.shape)
    grad_weights = jnp.einsum(
        "bqhe,bkhe->bhqk", grad_heads, value_rows, preferred_element_type=FLOAT
    )
    grad_value = jnp.einsum(
        "bhqk,bqhe->bkhe", weights.astype(BFLOAT), grad_heads, preferred_element_type=FLOAT
    )
    grad_scores = (
        weights * (grad_weights - jnp.sum(weights * grad_weights, axis=-1, keepdims=True))
    ).astype(BFLOAT)
    grad_query = jnp.einsum(
        "bhqk,bkhe->bqhe", grad_scores, key_rows, preferred_element_type=FLOAT
    ) * HEAD ** (-0.5)
    grad_key = jnp.einsum(
        "bhqk,bqhe->bkhe", grad_scores, query_rows, preferred_element_type=FLOAT
    ) * HEAD ** (-0.5)
    grad_projected = (
        jnp.stack([grad_query, grad_key, grad_value], axis=2)
        .reshape(projected_low.shape)
        .astype(BFLOAT)
    )
    input_grad = jnp.einsum(
        "bsd,bt,bsce->dtce", inputs_low, task_low, grad_projected, preferred_element_type=FLOAT
    )
    grad_hidden_zero = grad_residual_one + mixed_back(
        jnp.einsum(
            "bsce,dce->bsd", grad_projected, matrices[:, 0:3, :], preferred_element_type=FLOAT
        )
    )
    task_grads = jnp.concatenate(
        [input_grad, output_grad[:, :, None, :], up_grad, down_grad], axis=2
    )

    def own_block(full_array):
        return lax.dynamic_slice_in_dim(full_array, column_start, width_own, 0)

    projected_sums = jnp.sum(grad_projected, axis=(0, 1), dtype=FLOAT)
    front_rows = jnp.stack(
        [
            projected_sums[0],
            projected_sums[2],
            own_block(jnp.sum(grad_attended, axis=(0, 1), dtype=FLOAT)),
            own_block(gain_one),
            own_block(bias_one),
        ]
    )
    inner_rows = jnp.sum(grad_inner, axis=(0, 1), dtype=FLOAT)
    back_rows = jnp.stack(
        [
            own_block(jnp.sum(grad_branch, axis=(0, 1), dtype=FLOAT)),
            own_block(gain_two),
            own_block(bias_two),
        ]
    )
    return (grad_hidden_zero, task_grads, jnp.concatenate([front_rows, inner_rows, back_rows]))


def adam_update(weight, gradient, first_moment, second_moment, step_rate, weight_decay):
    moment_new = BETA_ONE * first_moment + (1.0 - BETA_ONE) * gradient
    square_new = BETA_TWO * second_moment + (1.0 - BETA_TWO) * gradient * gradient
    corrected = moment_new / (1.0 - BETA_ONE**STEP)
    scaled = square_new / (1.0 - BETA_TWO**STEP)
    weight_new = weight - step_rate * (
        corrected / (jnp.sqrt(scaled) + ADAM_EPS) + weight_decay * weight
    )
    return (moment_new, square_new, weight_new)


def on_device(
    token_ids,
    segment_ids,
    task_ids,
    task_order,
    counted,
    targets,
    word_table,
    word_first,
    word_second,
    tables,
    tables_first,
    tables_second,
    matrices,
    matrices_first,
    matrices_second,
    vectors,
    vectors_first,
    vectors_second,
    regressor,
    regressor_first,
    regressor_second,
):
    word_stored = word_table.shape
    matrix_stored = matrices.shape
    width_own = matrices.shape[1] // 12
    word_table = word_table.reshape(-1, width_own)
    word_first = word_first.reshape(-1, width_own)
    word_second = word_second.reshape(-1, width_own)
    matrices = matrices.reshape(matrices.shape[0], 12, width_own)
    matrices_first = matrices_first.reshape(matrices.shape)
    matrices_second = matrices_second.reshape(matrices.shape)
    task_number = regressor.shape[0]
    column_start = lax.axis_index("mp") * width_own
    slice_width = tables.shape[1]
    slice_start = lax.axis_index("dp") * slice_width
    batch_size, length = token_ids.shape
    word_all, matrix_all = (
        lax.all_gather(word_table.astype(BFLOAT), "dp", axis=0, tiled=True),
        lax.all_gather(matrices.astype(BFLOAT), "dp", axis=0, tiled=True),
    )
    table_all, vector_all, regressor_all = (
        lax.all_gather(tables.astype(BFLOAT), "dp", axis=1, tiled=True),
        lax.all_gather(vectors.astype(BFLOAT), "dp", axis=1, tiled=True),
        lax.all_gather(regressor.astype(BFLOAT), "dp", axis=1, tiled=True),
    )
    table_full = table_all.astype(FLOAT)
    vector_full = vector_all.astype(FLOAT)
    regressor_full = regressor_all.astype(FLOAT)
    full_width = vector_full.shape[1]
    vector_own = lax.dynamic_slice_in_dim(vector_full, column_start, width_own, 1)
    token_flat = token_ids.reshape(-1)
    looked = jnp.take(word_all, token_flat, axis=0)
    embedded_words = lax.all_gather(looked, "mp", axis=1, tiled=True).reshape(
        batch_size, length, full_width
    )
    segment_rows = jnp.where(
        segment_ids[:, :, None] == 1, table_full[length + 1], table_full[length]
    )
    embedded = embedded_words.astype(FLOAT) + table_full[:length] + segment_rows
    hidden_zero = layer_norm(embedded, vector_full[0], vector_full[1])
    hidden_two, saved_values = layer_forward(hidden_zero, matrix_all, vector_full, vector_own)
    task_hot = (task_ids[:, None] == jnp.arange(task_number, dtype=jnp.int32)[None, :]).astype(
        FLOAT
    )
    counted_float = counted.astype(FLOAT)
    predicted_all = jnp.einsum("bsd,td->bst", hidden_two, regressor_full, precision=HIGHEST)
    predicted = jnp.sum(predicted_all * task_hot[:, None, :], axis=-1)
    errors = (predicted - targets) * counted_float
    local_counts = jnp.sum(task_hot * jnp.sum(counted_float, axis=1)[:, None], axis=0)
    local_errors = jnp.sum(task_hot * jnp.sum(errors * errors, axis=1)[:, None], axis=0)
    task_counts, task_errors = lax.psum((local_counts, local_errors), "dp")
    loss_total = jnp.sum(task_errors / task_counts)
    grad_predicted = 2.0 * errors / jnp.dot(task_hot, task_counts, precision=HIGHEST)[:, None]
    grad_two = (
        grad_predicted[:, :, None]
        * jnp.dot(task_hot, regressor_full, precision=HIGHEST)[:, None, :]
    )
    grad_hidden_zero, per_task, layer_vector_grads = layer_backward(
        grad_two, matrix_all, vector_full, saved_values, column_start, task_hot.astype(BFLOAT)
    )
    norm_zero = jax.vjp(layer_norm, embedded, vector_full[0], vector_full[1])[1]
    grad_embedded, gain_zero, bias_zero = norm_zero(grad_hidden_zero)
    grad_own = lax.dynamic_slice_in_dim(grad_embedded, column_start, width_own, 2)
    word_rows = grad_own.astype(BFLOAT).reshape(batch_size * length, width_own)
    segment_one = segment_ids.astype(FLOAT)[:, :, None]
    table_own = jnp.concatenate(
        [
            jnp.sum(grad_own, axis=0),
            jnp.sum(grad_own * (1.0 - segment_one), axis=(0, 1))[None],
            jnp.sum(grad_own * segment_one, axis=(0, 1))[None],
        ]
    )
    hidden_own = lax.dynamic_slice_in_dim(hidden_two, column_start, width_own, 2)
    regressor_own = jnp.einsum(
        "bs,bsd,bt->td", grad_predicted, hidden_own, task_hot, precision=HIGHEST
    )
    embed_rows = jnp.stack(
        [
            lax.dynamic_slice_in_dim(gain_zero, column_start, width_own, 0),
            lax.dynamic_slice_in_dim(bias_zero, column_start, width_own, 0),
        ]
    )
    vector_own_grads = jnp.concatenate([embed_rows, layer_vector_grads])
    dense_words = (
        jnp.zeros((word_all.shape[0], width_own), FLOAT).at[token_flat].add(word_rows.astype(FLOAT))
    )
    task_slices, word_grad = (
        lax.psum_scatter(per_task, "dp", scatter_dimension=0, tiled=True),
        lax.psum_scatter(dense_words, "dp", scatter_dimension=0, tiled=True),
    )

    def spread(block_rows):
        return lax.dynamic_update_slice_in_dim(
            jnp.zeros((block_rows.shape[0], full_width), FLOAT), block_rows, column_start, 1
        )

    table_sum, vector_sum, regressor_sum = lax.psum(
        (spread(table_own), spread(vector_own_grads), spread(regressor_own)), ("dp", "mp")
    )
    task_norms = lax.psum(jnp.sum(task_slices * task_slices, axis=(0, 2, 3)), ("dp", "mp"))
    trunk_grad = jnp.zeros_like(task_slices[:, 0])
    for first_task in range(task_number):
        current = task_slices[:, first_task]
        for position in range(task_number):
            other_task = task_order[position]
            other_grad = jnp.take(task_slices, other_task, axis=1)
            inner_dot = lax.psum(jnp.sum(current * other_grad), ("dp", "mp"))
            factor = jnp.where(
                other_task == first_task, 0.0, jnp.minimum(inner_dot, 0.0) / task_norms[other_task]
            )
            current = current - factor * other_grad
        trunk_grad = trunk_grad + current
    small_squares = (
        jnp.sum(table_sum * table_sum)
        + jnp.sum(vector_sum * vector_sum)
        + jnp.sum(regressor_sum * regressor_sum)
    )
    local_squares = jnp.sum(trunk_grad * trunk_grad) + jnp.sum(word_grad * word_grad)
    grad_norm = jnp.sqrt(lax.psum(local_squares, ("dp", "mp")) + small_squares)
    clip_scale = jnp.minimum(1.0, CLIP / grad_norm)

    def own_columns(full_array):
        return lax.dynamic_slice_in_dim(full_array, slice_start, slice_width, 1)

    word_clipped = word_grad * clip_scale
    tables_clipped = own_columns(table_sum) * clip_scale
    matrices_clipped = trunk_grad * clip_scale
    vectors_clipped = own_columns(vector_sum) * clip_scale
    regressor_clipped = own_columns(regressor_sum) * clip_scale
    word_moment, word_square, word_weight = adam_update(
        word_table, word_clipped, word_first, word_second, RATE_WEIGHT, DECAY
    )
    tables_moment, tables_square, tables_weight = adam_update(
        tables, tables_clipped, tables_first, tables_second, RATE_WEIGHT, DECAY
    )
    matrices_moment, matrices_square, matrices_weight = adam_update(
        matrices, matrices_clipped, matrices_first, matrices_second, RATE_WEIGHT, DECAY
    )
    vectors_moment, vectors_square, vectors_weight = adam_update(
        vectors, vectors_clipped, vectors_first, vectors_second, RATE_VECTOR, 0.0
    )
    regressor_moment, regressor_square, regressor_weight = adam_update(
        regressor, regressor_clipped, regressor_first, regressor_second, RATE_WEIGHT, DECAY
    )
    return (
        word_clipped.reshape(word_stored),
        word_moment.reshape(word_stored),
        word_square.reshape(word_stored),
        word_weight.reshape(word_stored),
        tables_clipped,
        tables_moment,
        tables_square,
        tables_weight,
        matrices_clipped.reshape(matrix_stored),
        matrices_moment.reshape(matrix_stored),
        matrices_square.reshape(matrix_stored),
        matrices_weight.reshape(matrix_stored),
        vectors_clipped,
        vectors_moment,
        vectors_square,
        vectors_weight,
        regressor_clipped,
        regressor_moment,
        regressor_square,
        regressor_weight,
        grad_norm,
        loss_total,
        task_counts,
    )


def solution(mesh):
    placed = (
        P("dp", None),
        P("dp", None),
        P("dp"),
        P(),
        P("dp", None),
        P("dp", None),
        P("dp", "mp"),
        P("dp", "mp"),
        P("dp", "mp"),
        P(None, "dp"),
        P(None, "dp"),
        P(None, "dp"),
        P("dp", "mp"),
        P("dp", "mp"),
        P("dp", "mp"),
        P(None, "dp"),
        P(None, "dp"),
        P(None, "dp"),
        P(None, "dp"),
        P(None, "dp"),
        P(None, "dp"),
    )
    return jax.shard_map(
        on_device,
        mesh=mesh,
        in_specs=placed,
        out_specs=(
            P("dp", "mp"),
            P("dp", "mp"),
            P("dp", "mp"),
            P("dp", "mp"),
            P(None, "dp"),
            P(None, "dp"),
            P(None, "dp"),
            P(None, "dp"),
            P("dp", "mp"),
            P("dp", "mp"),
            P("dp", "mp"),
            P("dp", "mp"),
            P(None, "dp"),
            P(None, "dp"),
            P(None, "dp"),
            P(None, "dp"),
            P(None, "dp"),
            P(None, "dp"),
            P(None, "dp"),
            P(None, "dp"),
            P(),
            P(),
            P(),
        ),
        check_vma=False,
    )
```

profile of v0, /device:TPU:0, one launch (start us, length us, event | category | flops | bytes accessed | tf_op | source)
XLA Modules:
  0.0 3028.4 jit_solution(15303415555671833600)
XLA Ops:
  19.1 214.3 %all-gather.6.cloned.1.call-done = bf16[30720,192]{1,0:T(8,128)(2,1)} async-done(((bf16[3840,192]{1,0:T(8,128)(2,1)}), bf16[30720,192]{1,0:T(8,128)(2,1)}) %all-gather.6.cloned.1.call-update) | async-done | bytes 11796496 | tf_op jit(solution)/shard_map/all_gather | solution.py:252
  233.4 23.4 gather_fusion
  261.6 34.9 %all_gather.20 = bf16[514,768]{0,1:T(8,128)(2,1)S(1)} all-gather(bf16[514,96]{0,1:T(8,128)(2,1)S(1)} %convert_element_type.115), channel_id=1, replica_groups=mesh['dp'=8,'mp'=4] {'dp'}, dimensions={1}, use_global_device_ids=true | all-gather | bytes 888192 | tf_op jit(solution)/shard_map/all_gather | solution.py:256
  298.2 30.9 %all-gather = bf16[8,96,14]{1,2,0:T(8,128)(2,1)S(1)} all-gather(bf16[1,96,14]{1,2,0:T(8,128)(2,1)S(1)} %convert_bitcast_fusion), channel_id=1, replica_groups=mesh['dp'=8,'mp'=4] {'dp'}, dimensions={0}, use_global_device_ids=true | all-gather | bytes 24192 | tf_op jit(solution)/shard_map/all_gather | solution.py:257
  359.2 31.7 %all-gather.8.cloned.1.call-done = bf16[4096,768]{0,1:T(8,128)(2,1)} async-done(((bf16[4096,192]{0,1:T(8,128)(2,1)}), bf16[4096,768]{0,1:T(8,128)(2,1)}) %all-gather.8.cloned.1.call-update) | async-done | bytes 6291472 | tf_op jit(solution)/shard_map/all_gather | solution.py:267
  476.2 209.7 %all-reduce.13.cloned.1.call-done = f32[8,512,768]{2,1,0:T(8,128)} async-done(((f32[8,512,768]{2,1,0:T(8,128)}), f32[8,512,768]{2,1,0:T(8,128)}) %all-reduce.13.cloned.1.call-update) | async-done | bytes 12582928 | tf_op jit(solution)/shard_map/psum | solution.py:35
  686.0 13.6 add_add_fusion.4
  724.5 32.2 %multiply_convert_fusion.1 = (bf16[8,512,4,192]{1,3,2,0:T(8,128)(2,1)S(1)}, f32[8,512,4,192]{1,3,2,0:T(8,128)}) fusion(f32[8,512,4,192]{1,3,2,0:T(8,128)} %get-tuple-element.251, f32[4,192]{1,0:T(4,128)S(1)} %slice.175, u8[512,4,192]{0,2,1:T(8,128)(4,1)S(1)} %get-tuple-element.137, u8[512,4,192]{0,2,1:T(8,128)(4,1)S(1)} %get-tuple-element.136), kind=kLoop, calls=%fused_computation.45 | loop fusion | flops 223346688 | bytes 32246784 | tf_op jit(solution)/shard_map/convert_element_type | solution.py:81
  768.0 20.5 all-gather.1
  789.0 199.4 %all-reduce.15.cloned.1.call-done = f32[8,512,768]{2,1,0:T(8,128)} async-done(((f32[8,512,768]{2,1,0:T(8,128)}), f32[8,512,768]{2,1,0:T(8,128)}) %all-reduce.15.cloned.1.call-update) | async-done | bytes 12582928 | tf_op jit(solution)/shard_map/psum | solution.py:35
  1009.0 22.3 all-reduce.6
  1052.8 17.8 convert_reduce_fusion.1
  1118.9 179.6 %all-reduce.17.cloned.1.call-done = f32[8,512,768]{2,1,0:T(8,128)} async-done(((f32[8,512,768]{2,1,0:T(8,128)}), f32[8,512,768]{2,1,0:T(8,128)}) %all-reduce.17.cloned.1.call-update) | async-done | bytes 12582928 | tf_op jit(solution)/shard_map/psum | solution.py:39
  1298.4 17.0 multiply_reduce_fusion.3
  1344.4 20.4 multiply_reduce_fusion
  1364.8 21.2 multiply_convert_fusion
  1449.7 19.8 pad_maximum_fusion
  1469.5 46.7 %copy.198 = f32[768,4,12,192]{3,2,1,0:T(8,128)} copy(f32[768,4,12,192]{0,1,3,2:T(4,128)} %pad_maximum_fusion) | data formatting | bytes 56623104
  1516.3 42.3 %reshape.485 = f32[768,9216]{1,0:T(8,128)} reshape(f32[768,4,12,192]{3,2,1,0:T(8,128)} %copy.198) | data formatting | bytes 56623104
  1559.3 73.0 %all-reduce.19.cloned.1.call-done = f32[8,512,768]{2,1,0:T(8,128)} async-done(((f32[8,512,768]{2,1,0:T(8,128)}), f32[8,512,768]{2,1,0:T(8,128)}) %all-reduce.19.cloned.1.call-update) | async-done | bytes 12582928 | tf_op jit(solution)/shard_map/psum | solution.py:39
  1632.2 19.3 multiply_reduce_fusion.4
  1676.3 35.8 %scatter_custom_fusion = f32[30720,192]{1,0:T(8,128)} fusion(s32[4096]{0:T(1024)} %bitcast.411, f32[]{:T(128)} %constant.71.clone.1, bf16[4096,192]{1,0:T(8,128)(2,1)S(1)} %bitcast.389), kind=kCustom, calls=%fused_computation.22 | custom fusion | flops 1572864 | bytes 25166336 | tf_op jit(solution)/shard_map/scatter-add | solution.py:319
  1767.3 317.9 %reduce-scatter.7.cloned.1.call-done = f32[96,9216]{1,0:T(8,128)} async-done(((f32[768,9216]{1,0:T(8,128)}), f32[96,9216]{1,0:T(8,128)}) %reduce-scatter.7.cloned.1.call-update) | async-done | bytes 3538960
  2096.3 486.6 %reduce-scatter.5.cloned.1.call-done = f32[3840,192]{1,0:T(8,128)} async-done(((f32[30720,192]{1,0:T(8,128)}), f32[3840,192]{1,0:T(8,128)}) %reduce-scatter.5.cloned.1.call-update) | async-done | bytes 2949136 | tf_op jit(solution)/shard_map/reduce_scatter | solution.py:323
  2586.6 39.8 %all-reduce.5 = (f32[]{:T(128)}, f32[4]{0:T(128)S(1)}) all-reduce(f32[]{:T(128)} %fusion.91, f32[4]{0:T(128)S(1)} %multiply_reduce_fusion.10), channel_id=1, replica_groups=mesh['dp'=8,'mp'=4] {'dp','mp'}, use_global_device_ids=true, to_apply=%region_27.29 | all-reduce | flops 5 | bytes 40 | tf_op jit(solution)/shard_map/psum | solution.py:341
  2631.3 40.3 %psum.196 = f32[]{:T(128)} all-reduce(f32[]{:T(128)} %get-tuple-element.221), channel_id=1, replica_groups=mesh['dp'=8,'mp'=4] {'dp','mp'}, use_global_device_ids=true, to_apply=%region_31.33 | all-reduce | flops 1 | bytes 8 | tf_op jit(solution)/shard_map/psum | solution.py:341
  2677.4 41.0 %all-reduce.4 = (f32[]{:T(128)}, f32[]{:T(128)}, f32[]{:T(128)}, f32[]{:T(128)}) all-reduce(f32[]{:T(128)} %get-tuple-element.152, f32[]{:T(128)} %get-tuple-element.151, f32[]{:T(128)} %get-tuple-element.149, f32[]{:T(128)} %get-tuple-element.150), channel_id=1, replica_groups=mesh['dp'=8,'mp'=4] {'dp','mp'}, use_global_device_ids=true, to_apply=%region_33.35 | all-reduce | flops 4 | bytes 32 | tf_op jit(solution)/shard_map/psum | solution.py:341
  2730.7 40.1 %psum.200 = f32[]{:T(128)} all-reduce(f32[]{:T(128)} %get-tuple-element.143), channel_id=1, replica_groups=mesh['dp'=8,'mp'=4] {'dp','mp'}, use_global_device_ids=true, to_apply=%region_39.41 | all-reduce | flops 1 | bytes 8 | tf_op jit(solution)/shard_map/psum | solution.py:341
  2774.7 40.7 %all-reduce.3 = (f32[]{:T(128)}, f32[]{:T(128)}, f32[]{:T(128)}) all-reduce(f32[]{:T(128)} %fusion.77, f32[]{:T(128)} %get-tuple-element.141, f32[]{:T(128)} %get-tuple-element.142), channel_id=1, replica_groups=mesh['dp'=8,'mp'=4] {'dp','mp'}, use_global_device_ids=true, to_apply=%region_41.43 | all-reduce | flops 3 | bytes 24 | tf_op jit(solution)/shard_map/psum | solution.py:341
  2823.8 40.2 %all-reduce.2 = (f32[]{:T(128)}, f32[]{:T(128)}) all-reduce(f32[]{:T(128)} %get-tuple-element.146, f32[]{:T(128)} %get-tuple-element.145), channel_id=1, replica_groups=mesh['dp'=8,'mp'=4] {'dp','mp'}, use_global_device_ids=true, to_apply=%region_49.51 | all-reduce | flops 2 | bytes 16 | tf_op jit(solution)/shard_map/psum | solution.py:341
  2870.9 40.8 %all-reduce.1 = (f32[]{:T(128)}, f32[]{:T(128)}, f32[]{:T(128)}, f32[]{:T(128)}) all-reduce(f32[]{:T(128)} %get-tuple-element.148, f32[]{:T(128)} %get-tuple-element.147, f32[]{:T(128)} %get-tuple-element.144, f32[]{:T(128)} %get-tuple-element.140), channel_id=1, replica_groups=mesh['dp'=8,'mp'=4] {'dp','mp'}, use_global_device_ids=true, to_apply=%region_59.61 | all-reduce | flops 4 | bytes 32 | tf_op jit(solution)/shard_map/psum | solution.py:341
  2925.6 41.2 %all-reduce = (f32[]{:T(128)}, f32[14,768]{1,0:T(8,128)S(1)}, f32[4,768]{1,0:T(4,128)S(1)}) all-reduce(f32[]{:T(128)S(6)} %add.416, f32[14,768]{1,0:T(8,128)} %dynamic_update_slice.10, f32[4,768]{1,0:T(4,128)S(1)} %dynamic_update_slice.11), channel_id=1, replica_groups=mesh['dp'=8,'mp'=4] {'dp','mp'}, use_global_device_ids=true, to_apply=%region_62.64 | all-reduce | flops 13825 | bytes 110600 | tf_op jit(solution)/shard_map/psum | solution.py:353
  (372 shorter events, 513.9 us)
Async XLA Ops:
  7.2 226.2 %all-gather.6.cloned.1.call-start = ((), (), s32[]{:S(2)}) async-start(), calls=%async_computation.2 | async-start | bytes 17694720 | tf_op jit(solution)/shard_map/all_gather | solution.py:252
  15.7 335.2 %all-gather.10.cloned.1.call-start = ((), (), s32[]{:S(2)}) async-start(), calls=%async_computation.4 | async-start | bytes 7077888 | tf_op jit(solution)/shard_map/all_gather | solution.py:253
  16.1 240.7 %copy-start.16 = (f32[96,2304]{0,1:T(8,128)}, f32[96,2304]{0,1:T(8,128)S(1)}, u32[]{:S(2)}) copy-start(f32[96,2304]{0,1:T(8,128)S(1)} %copy.158) | copy-start | bytes 2654212
  18.3 372.6 %all-gather.8.cloned.1.call-start = ((), (), s32[]{:S(2)}) async-start(), calls=%async_computation.3 | async-start | bytes 7864320 | tf_op jit(solution)/shard_map/all_gather | solution.py:267
  256.8 41.3 %copy-start.45 = (s32[8,512]{1,0:T(8,128)S(1)}, s32[8,512]{1,0:T(8,128)}, u32[]{:S(2)}) copy-start(s32[8,512]{1,0:T(8,128)} %param.24) | copy-start | bytes 49156
  256.8 41.4 %copy-start.74 = (f32[14,96]{1,0:T(8,128)S(1)}, f32[14,96]{1,0:T(8,128)}, u32[]{:S(2)}) copy-start(f32[14,96]{1,0:T(8,128)} %param.38) | copy-start | bytes 16132
  261.5 424.4 %all-reduce.13.cloned.1.call-start = ((), (), s32[]{:S(2)}) async-start(), calls=%async_computation.5 | async-start | bytes 25165824 | tf_op jit(solution)/shard_map/psum | solution.py:35
  329.7 356.3 %copy-start.7 = (f32[512,768]{1,0:T(8,128)}, f32[512,768]{1,0:T(8,128)S(1)}, u32[]{:S(2)}) copy-start(f32[512,768]{1,0:T(8,128)S(1)} %copy.155) | copy-start | bytes 4718596
  349.2 336.8 %copy-start.65 = (f32[768]{0:T(1024)}, f32[768]{0:T(1024)S(1)}, u32[]{:S(2)}) copy-start(f32[768]{0:T(1024)S(1)} %get-tuple-element.162) | copy-start | bytes 9220
  349.2 336.8 %copy-start.77 = (f32[768]{0:T(1024)}, f32[768]{0:T(1024)S(1)}, u32[]{:S(2)}) copy-start(f32[768]{0:T(1024)S(1)} %get-tuple-element.161) | copy-start | bytes 9220
  350.7 335.2 %copy-start.58 = (f32[768]{0:T(1024)}, f32[768]{0:T(1024)S(1)}, u32[]{:S(2)}) copy-start(f32[768]{0:T(1024)S(1)} %get-tuple-element.153) | copy-start | bytes 9220
  350.7 335.2 %copy-start.60 = (f32[768]{0:T(1024)}, f32[768]{0:T(1024)S(1)}, u32[]{:S(2)}) copy-start(f32[768]{0:T(1024)S(1)} %get-tuple-element.154) | copy-start | bytes 9220
  350.9 335.1 %copy-start.67 = (pred[8,512]{1,0:T(8,128)(4,1)}, pred[8,512]{1,0:T(8,128)(4,1)S(1)}, u32[]{:S(2)}) copy-start(pred[8,512]{1,0:T(8,128)(4,1)S(1)} %broadcast_compare_fusion) | copy-start | bytes 12292
  354.5 102.9 %copy-start.34 = (bf16[768,1,192]{0,2,1:T(8,128)(2,1)}, bf16[768,1,192]{0,2,1:T(8,128)(2,1)S(1)}, u32[]{:S(2)}) copy-start(bf16[768,1,192]{0,2,1:T(8,128)(2,1)S(1)} %copy.203) | copy-start | bytes 884740
  398.6 287.3 %copy-start.47 = (f32[8,512]{1,0:T(8,128)}, f32[8,512]{1,0:T(8,128)S(1)}, u32[]{:S(2)}) copy-start(f32[8,512]{1,0:T(8,128)S(1)} %div.200) | copy-start | bytes 49156
  407.4 278.6 %copy-start.49 = (f32[8,512]{1,0:T(8,128)}, f32[8,512]{1,0:T(8,128)S(1)}, u32[]{:S(2)}) copy-start(f32[8,512]{1,0:T(8,128)S(1)} %rsqrt.33) | copy-start | bytes 49156
  465.1 523.3 %all-reduce.15.cloned.1.call-start = ((), (), s32[]{:S(2)}) async-start(), calls=%async_computation.6 | async-start | bytes 25165824 | tf_op jit(solution)/shard_map/psum | solution.py:35
  724.5 34.8 %copy-start.32 = (bf16[768,4,192]{0,2,1:T(8,128)(2,1)S(1)}, bf16[768,4,192]{0,2,1:T(8,128)(2,1)}, u32[]{:S(2)}) copy-start(bf16[768,4,192]{0,2,1:T(8,128)(2,1)} %copy.205) | copy-start | bytes 3538948
  767.3 21.4 copy-start.73
  767.3 221.1 %copy-start.80 = (f32[768]{0:T(1024)S(1)}, f32[768]{0:T(1024)}, u32[]{:S(2)}) copy-start(f32[768]{0:T(1024)} %get-tuple-element.156) | copy-start | bytes 9220
  767.4 531.1 %all-reduce.17.cloned.1.call-start = ((), (), s32[]{:S(2)}) async-start(), calls=%async_computation.7 | async-start | bytes 25165824 | tf_op jit(solution)/shard_map/psum | solution.py:39
  1031.4 267.0 %copy-start.43 = (f32[8,512]{1,0:T(8,128)}, f32[8,512]{1,0:T(8,128)S(1)}, u32[]{:S(2)}) copy-start(f32[8,512]{1,0:T(8,128)S(1)} %multiply_divide_fusion) | copy-start | bytes 49156
  1081.1 551.2 %all-reduce.19.cloned.1.call-start = ((), (), s32[]{:S(2)}) async-start(), calls=%async_computation.8 | async-start | bytes 25165824 | tf_op jit(solution)/shard_map/psum | solution.py:39
  1118.9 196.6 %copy-start.54 = (f32[8,512]{1,0:T(8,128)S(1)}, f32[8,512]{1,0:T(8,128)}, u32[]{:S(2)}) copy-start(f32[8,512]{1,0:T(8,128)} %copy-done.53) | copy-start | bytes 49156
  1364.7 21.2 copy-start.15
  1411.2 674.0 %reduce-scatter.7.cloned.1.call-start = ((), (), s32[]{:S(2)}) async-start(), calls=%async_computation.11 | async-start | bytes 31850496
  1558.5 73.7 %copy-start.63 = (f32[8,512]{1,0:T(8,128)S(1)}, f32[8,512]{1,0:T(8,128)}, u32[]{:S(2)}) copy-start(f32[8,512]{1,0:T(8,128)} %copy-done.62) | copy-start | bytes 49156
  1558.6 1024.3 %reduce-scatter.5.cloned.1.call-start = ((), (), s32[]{:S(2)}) async-start(), calls=%async_computation.9 | async-start | bytes 35389440 | tf_op jit(solution)/shard_map/reduce_scatter | solution.py:323
  1559.3 92.3 %copy-start.56 = (f32[8,512]{1,0:T(8,128)S(1)}, f32[8,512]{1,0:T(8,128)}, u32[]{:S(2)}) copy-start(f32[8,512]{1,0:T(8,128)} %copy-done.55) | copy-start | bytes 49156
  1712.0 20.8 copy-start.42
  1712.1 1210.9 %all-reduce.21.cloned.1.call-start = ((), (), s32[]{:S(2)}) async-start(), calls=%async_computation.10 | async-start | bytes 3932160 | tf_op jit(solution)/shard_map/psum | solution.py:331
  2631.3 92.5 %copy-start.18 = (f32[96,12,192]{0,2,1:T(8,128)}, f32[96,12,192]{0,2,1:T(8,128)S(1)}, u32[]{:S(2)}) copy-start(f32[96,12,192]{0,2,1:T(8,128)S(1)} %get-tuple-element.222) | copy-start | bytes 2654212
  (70 other events, 663.6 us)
Sparse Core Ops, SparseCore 0:
  15.8 217.4 all-gather.5
  236.1 106.6 all-gather.9
  345.0 45.8 all-gather.7
  465.2 220.6 all-reduce.12
  767.5 220.8 all-reduce.14
  1081.2 217.2 all-reduce.16
  1411.3 220.8 all-reduce.18
  1636.2 448.9 reduce-scatter.6
  2089.6 493.2 reduce-scatter.4
  2589.5 132.6 all-reduce.20
where the time goes:
time: 3040 us; the launch traced here: 3030 us
  waiting for transfers between devices  1710 us (56%)
  blocking collectives  433 us (14%)
  other arithmetic  349 us (11%)
  local copies, waits for them, and re-layouts  243 us (8%)
  matrix products  230 us (8%)
  between operations  60.4 us (2%)
    reduce_scatter x1, waiting for transfers between devices, on_device(): lax.psum_scatter(dense_words, 'dp', scatter_dimension=0, tiled=True)  487 us
    psum x2, waiting for transfers between devices, mixed_sum(): return lax.psum(partial_value, 'mp')  409 us
    unnamed x11, waiting for transfers between devices  318 us
    psum x7, blocking collectives, on_device(): inner_dot = lax.psum(jnp.sum(current * other_grad), ('dp', 'mp'))  283 us
    psum x2, waiting for transfers between devices, mixed_back(): return lax.psum(partial_value, 'mp')  253 us
    all_gather x1, waiting for transfers between devices, on_device(): lax.all_gather(word_table.astype(BFLOAT), 'dp', axis=0, tiled=True)  214 us
    unnamed x203, local copies, waits for them, and re-layouts  134 us
  transfers between devices with their start and end apart: 10, of which 8 were waited for; matrix products, arithmetic and copies ran while one was open for 14% of the time, Pallas kernels for 0%

commit v1 on v0

v1 whole, which is shorter than its diff:
```python
import functools

import jax
import jax.numpy as jnp
from jax import lax
from jax.experimental import pallas as pl
from jax.experimental.pallas import tpu as pltpu
from jax.sharding import PartitionSpec as P

HEAD = 64
STEP = 5


HIGHEST = lax.Precision.HIGHEST
FLOAT = jnp.float32
BFLOAT = jnp.bfloat16
NORM_EPS = 1e-12
CLIP = 0.05
BETA_ONE = 0.9
BETA_TWO = 0.999
ADAM_EPS = 1e-08
RATE_WEIGHT = 0.03
RATE_VECTOR = 0.3
DECAY = 0.01


def layer_norm(inputs, norm_gain, norm_bias):
    center = jnp.mean(inputs, axis=-1, keepdims=True)
    offset = inputs - center
    spread = jnp.mean(offset * offset, axis=-1, keepdims=True)
    return offset * lax.rsqrt(spread + NORM_EPS) * norm_gain + norm_bias


def gelu_exact(inputs):
    return jax.nn.gelu(inputs, approximate=False)


MIB = 1 << 20
CHEAP = pl.CostEstimate(flops=1, bytes_accessed=1, transcendentals=0)
ROOT_HALF = 0.5**0.5
BELL = (2.0 * 3.141592653589793) ** -0.5
CONTRACT_LAST = (((1,), (1,)), ((), ()))
CONTRACT_FIRST = (((0,), (0,)), ((), ()))
CONTRACT_CROSS = (((0,), (1,)), ((), ()))


def matmul(left, right, dims=(((1,), (0,)), ((), ()))):
    return lax.dot_general(left, right, dims, preferred_element_type=FLOAT)


def softmax_down(query, keys):
    scores = matmul(keys, query, CONTRACT_LAST) * HEAD ** (-0.5)
    powers = jnp.exp(scores - jnp.max(scores, axis=0, keepdims=True))
    return powers * (1.0 / jnp.sum(powers, axis=0, keepdims=True))


def add_over_steps(step, out_ref, part):
    @pl.when(step == 0)
    def _():
        out_ref[0] = part

    @pl.when(step > 0)
    def _():
        out_ref[0] = out_ref[0] + part


def attention_forward_kernel(order_ref, low_ref, weight_ref, bias_ref, saved_ref, attended_ref):
    width = weight_ref.shape[2] // 4
    heads = width // HEAD
    cut, pad = 3 * width - HEAD, HEAD
    projected = matmul(low_ref[0], weight_ref[0]) + bias_ref[0]
    low = projected.astype(BFLOAT)
    parts = [jnp.zeros((pad, low.shape[0]), FLOAT)]
    for head in range(heads):
        query, keys, values = [
            low[:, c * width + head * HEAD : c * width + (head + 1) * HEAD] for c in range(3)
        ]
        weights = softmax_down(query, keys).astype(BFLOAT)
        parts.append(matmul(values, weights, CONTRACT_FIRST))
    context = jnp.concatenate(parts, axis=0).T.astype(BFLOAT)
    lane = lax.broadcasted_iota(jnp.int32, context.shape, 1)
    saved_ref[0, 0, :, :cut] = low[:, :cut]
    saved_ref[0, 0, :, cut:] = jnp.where(lane < pad, low[:, cut:], context)
    add_over_steps(
        pl.program_id(1), attended_ref, matmul(context, weight_ref[0, :, cut:], CONTRACT_LAST)
    )


def norm_parts(values):
    center = jnp.mean(values, axis=-1, keepdims=True)
    offset = values - center
    inverse = lax.rsqrt(jnp.mean(offset * offset, axis=-1, keepdims=True) + NORM_EPS)
    return offset * inverse, inverse


def norm_back(normed, inverse, gain, grad):
    scaled = grad * gain
    mean = jnp.mean(scaled, axis=-1, keepdims=True)
    along = jnp.mean(scaled * normed, axis=-1, keepdims=True)
    sums = [jnp.sum(grad * normed, axis=0, keepdims=True), jnp.sum(grad, axis=0, keepdims=True)]
    return inverse * (scaled - mean - normed * along), sums


def store_rows(out_ref, rows):
    out_ref[0] = jnp.zeros(out_ref.shape[1:], FLOAT)
    for index, row in enumerate(rows):
        out_ref[0, index : index + 1] = row


def store_half(step, other_ref, own_ref, value, total_ref):
    for index in range(2):

        @pl.when(step == index)
        def _():
            other_ref[index][0] = value

    @pl.when(step >= 2)
    def _():
        own_ref[0, 0] = value

    if total_ref is not None:
        total = jnp.sum(value.astype(FLOAT), axis=0, keepdims=True)
        total_ref[0, 0] = jnp.broadcast_to(total, total_ref.shape[2:])


def add_step(step, sum_ref, part):
    @pl.when(step == 0)
    def _():
        sum_ref[...] = part

    @pl.when(step > 0)
    def _():
        sum_ref[...] = sum_ref[...] + part


def attention_backward_kernel(
    order_ref, saved_ref, weight_ref, grad_ref, residual_ref, embedded_ref, segment_ref, vector_ref,
    other0_ref, other1_ref, own_ref, total_ref, words_ref, tables_ref, sums_ref, through,
):
    width = weight_ref.shape[2] // 4
    heads = width // HEAD
    cut, pad = 3 * width - HEAD, HEAD
    low = saved_ref[0, 0]
    grad_context = matmul(grad_ref[0], weight_ref[0, :, cut:]).astype(BFLOAT)
    grads = [[], [], []]
    for head in range(heads):
        query, keys, values = [
            low[:, c * width + head * HEAD : c * width + (head + 1) * HEAD] for c in range(3)
        ]
        grad_head = grad_context[:, pad + head * HEAD : pad + (head + 1) * HEAD]
        probs = softmax_down(query, keys)
        grad_weights = matmul(values, grad_head, CONTRACT_LAST)
        weighted = probs * grad_weights
        total = jnp.sum(weighted, axis=0, keepdims=True)
        grad_scores = (weighted - probs * total).astype(BFLOAT)
        grads[0].append(matmul(keys, grad_scores, CONTRACT_FIRST) * HEAD ** (-0.5))
        grads[1].append(matmul(query, grad_scores, CONTRACT_CROSS) * HEAD ** (-0.5))
        grads[2].append(matmul(grad_head, probs.astype(BFLOAT), CONTRACT_CROSS))
    blank = [jnp.zeros((pad, low.shape[0]), FLOAT)]
    turned = jnp.concatenate(grads[0] + grads[1] + grads[2] + blank, axis=0).T.astype(BFLOAT)
    span = 3 * width + pad
    lane = lax.broadcasted_iota(jnp.int32, (low.shape[0], 4 * width - cut), 1)
    tail = jnp.concatenate([turned[:, cut:], low[:, span:]], axis=1)
    tail = jnp.where(lane < pad, tail, low[:, cut:])
    step = pl.program_id(1)
    store_half(step, (other0_ref, other1_ref), own_ref, jnp.concatenate([turned[:, :cut], tail], axis=1), total_ref)
    add_step(step, through, matmul(turned, weight_ref[0, :, :span], CONTRACT_LAST))

    @pl.when(step == pl.num_programs(1) - 1)
    def _():
        normed, inverse = norm_parts(embedded_ref[0])
        grad = residual_ref[0] + through[...]
        grad_embedded, rows = norm_back(normed, inverse, vector_ref[0:1], grad)
        grad_low = grad_embedded.astype(BFLOAT)
        for group in range(words_ref.shape[0]):
            words_ref[group, 0] = grad_low[:, group * width : (group + 1) * width]
        second = segment_ref[0].astype(FLOAT)
        rows.append(jnp.sum(grad_embedded * (1.0 - second), axis=0, keepdims=True))
        rows.append(jnp.sum(grad_embedded * second, axis=0, keepdims=True))
        store_rows(sums_ref, rows)
        add_step(pl.program_id(0), tables_ref, grad_embedded)


def feed_forward_kernel(
    order_ref, zero_ref, attended_ref, up_ref, down_ref, bias_ref, vector_ref, head_ref, target_ref,
    other0_ref, other1_ref, own_ref, slope_ref, residual_ref, low_ref, grad_ref, grad_low_ref, sums_ref,
    hidden, fed,
):
    step = pl.program_id(1)

    @pl.when(step == 0)
    def _():
        residual = zero_ref[0] + (attended_ref[0] + vector_ref[4:5])
        residual_ref[0] = residual
        hidden[...] = norm_parts(residual)[0] * vector_ref[5:6] + vector_ref[6:7]
        low_ref[0] = hidden[...].astype(BFLOAT)

    inner = matmul(low_ref[0], up_ref[0]) + bias_ref[0]
    share = 0.5 + 0.5 * lax.erf(inner * ROOT_HALF)
    slope_ref[0, 0] = share + inner * (BELL * jnp.exp(-0.5 * inner * inner))
    active = (inner * share).astype(BFLOAT)
    store_half(step, (other0_ref, other1_ref), own_ref, active, None)
    add_step(step, fed, matmul(active, down_ref[0], CONTRACT_LAST))

    @pl.when(step == pl.num_programs(1) - 1)
    def _():
        normed, inverse = norm_parts(hidden[...] + (fed[...] + vector_ref[11:12]))
        hidden_two = normed * vector_ref[12:13] + vector_ref[13:14]
        row = head_ref[0, 0:1]
        predicted = jnp.sum(hidden_two * row, axis=1, keepdims=True)
        errors = (predicted - target_ref[0, :, 0:1]) * target_ref[0, :, 1:2]
        grad_predicted = errors * head_ref[0, 1:2, 0:1]
        grad_residual, rows = norm_back(normed, inverse, vector_ref[12:13], grad_predicted * row)
        grad_ref[0] = grad_residual
        grad_low = grad_residual.astype(BFLOAT)
        grad_low_ref[0] = grad_low
        rows.append(jnp.sum(grad_low.astype(FLOAT), axis=0, keepdims=True))
        rows.append(jnp.sum(grad_predicted * hidden_two, axis=0, keepdims=True))
        squares = jnp.sum(errors * errors, axis=0, keepdims=True)
        rows.append(jnp.broadcast_to(squares, rows[0].shape))
        store_rows(sums_ref, rows)


def feed_backward_kernel(
    order_ref, grad_low_ref, slope_ref, up_ref, down_ref, grad_ref, residual_ref, vector_ref,
    other0_ref, other1_ref, own_ref, total_ref, grad_one_ref, grad_one_low_ref, sums_ref, through,
):
    grad_active = matmul(grad_low_ref[0], down_ref[0])
    grad_inner = (grad_active * slope_ref[0, 0]).astype(BFLOAT)
    step = pl.program_id(1)
    store_half(step, (other0_ref, other1_ref), own_ref, grad_inner, total_ref)
    add_step(step, through, matmul(grad_inner, up_ref[0], CONTRACT_LAST))

    @pl.when(step == pl.num_programs(1) - 1)
    def _():
        normed, inverse = norm_parts(residual_ref[0])
        grad = grad_ref[0] + through[...]
        grad_residual, rows = norm_back(normed, inverse, vector_ref[5:6], grad)
        grad_one_ref[0] = grad_residual
        grad_low = grad_residual.astype(BFLOAT)
        grad_one_low_ref[0] = grad_low
        rows.append(jnp.sum(grad_low.astype(FLOAT), axis=0, keepdims=True))
        store_rows(sums_ref, rows)


def over_groups(body, order, inputs, outputs, scratch=()):
    examples, length, _ = next(value for kind, value in inputs if kind == "rows").shape

    def spec(kind, shape):
        if kind == "whole":
            return pl.BlockSpec(shape, lambda e, j, o: (0,) * len(shape))
        if kind == "words":
            return pl.BlockSpec((shape[0], 1) + shape[2:], lambda e, j, o: (0, e, 0, 0))
        if kind == "rows":
            return pl.BlockSpec((1,) + shape[1:], lambda e, j, o: (e, 0, 0))
        if kind == "group":
            return pl.BlockSpec((1,) + shape[1:], lambda e, j, o: (o[j], 0, 0))
        if kind in ("group left", "group right"):
            side = int(kind == "group right")
            return pl.BlockSpec(
                (1, shape[1], shape[2] // 2), lambda e, j, o, side=side: (o[j], 0, side)
            )
        if kind == "steps":
            return pl.BlockSpec((1, 1) + shape[2:], lambda e, j, o: (j, e, 0, 0))
        return pl.BlockSpec((1, 1) + shape[2:], lambda e, j, o: (jnp.maximum(j - 2, 0), e, 0, 0))

    return pl.pallas_call(
        body,
        grid_spec=pltpu.PrefetchScalarGridSpec(
            num_scalar_prefetch=1,
            grid=(examples, order.shape[0]),
            in_specs=[spec(kind, value.shape) for kind, value in inputs],
            out_specs=[spec(kind, value.shape) for kind, value in outputs],
            scratch_shapes=scratch,
        ),
        out_shape=[value for _, value in outputs],
        compiler_params=pltpu.CompilerParams(vmem_limit_bytes=56 * MIB),
        cost_estimate=pl.CostEstimate(flops=1, bytes_accessed=1, transcendentals=0),
    )(order, *[value for _, value in inputs])


X_BIT = 0


def place_of_piece(order, relative):
    index, weight = 0, 0
    for bit in order[1:]:
        index *= 2
        weight *= 2
        if bit == X_BIT:
            weight = 1
        else:
            index += int(bool(relative & bit))
    return bool(relative & order[0]), index, weight


def task_outer_kernel(pairs, mixed, orders, place_ref, *refs):
    count = (3 if mixed else 2) * pairs + 1
    inputs, outputs, sums = refs[:count], refs[count:-1], refs[-1]
    tasks, rows, width = sums.shape
    examples = inputs[0].shape[0]
    blocks = outputs[0].shape[0]
    block = outputs[0].shape[2]
    half = width // 2
    split = 3 * width // 4
    aligned = split // 256 * 256
    sums[...] = jnp.zeros_like(sums)
    for pair in range(pairs):
        left_ref = inputs[pair]
        for example in range(examples):
            task = place_ref[pair * examples + example]
            if pair == 0:
                right = inputs[pairs][0, example]
            else:
                right = jnp.where(
                    pl.program_id(0) == 0, inputs[pairs + 1][example], inputs[pairs + 2][example]
                )
            product = matmul(left_ref[example], right, CONTRACT_FIRST)
            if mixed:
                tail = matmul(inputs[2 * pairs + 1 + pair][example], right[:, aligned:], CONTRACT_FIRST)
                lane = lax.broadcasted_iota(jnp.int32, tail.shape, 1) + aligned
                tail = jnp.where(lane >= split, tail, product[:, aligned:])
                sums[task, :, :aligned] = sums[task, :, :aligned] + product[:, :aligned]
                sums[task, :, aligned:] = sums[task, :, aligned:] + tail
            else:
                sums[task] = sums[task] + product
    step = pl.program_id(0)
    own = place_ref[pairs * examples]

    def store(ref, index, task, part):
        ref[index, task] = part

    for relative in range(blocks):
        start = pl.multiple_of(lax.bitwise_xor(own, relative) * block, 8)
        for task in range(tasks):
            part = sums[task, pl.ds(start, block), :].astype(BFLOAT)
            for side, order in enumerate(orders):
                send_ref, keep_ref = outputs[2 * side : 2 * side + 2]
                piece = part[:, side * half : (side + 1) * half]
                sent, index, weight = place_of_piece(order, relative)
                if order[0] == X_BIT:
                    pl.when(step == 0)(functools.partial(store, send_ref, index, task, piece))
                    pl.when(step == 1)(functools.partial(store, keep_ref, index, task, piece))
                else:
                    store(send_ref if sent else keep_ref, index + (1 - step) * weight, task, piece)


def task_outer(place, lefts, rights, tasks, blocks, orders, others=()):
    examples, length, rows = lefts[0].shape
    width = rights[0].shape[3]
    pairs = len(lefts)
    once = pl.BlockSpec((examples, length, rows), lambda s, p: (0, 0, 0), pipeline_mode=pl.Buffered(1))
    right_spec = pl.BlockSpec((1, examples, length, width), lambda s, p: (s, 0, 0, 0))
    right_once = pl.BlockSpec((examples, length, width), lambda s, p: (0, 0, 0), pipeline_mode=pl.Buffered(1))
    shape = (blocks, tasks, rows // blocks, width // 2)
    out = jax.ShapeDtypeStruct(shape, BFLOAT)
    whole = pl.BlockSpec(shape, lambda s, p: (0, 0, 0, 0), pipeline_mode=pl.Buffered(1))
    sent0, kept0, sent1, kept1 = pl.pallas_call(
        functools.partial(task_outer_kernel, pairs, bool(others), orders),
        grid_spec=pltpu.PrefetchScalarGridSpec(
            num_scalar_prefetch=1,
            grid=(2,),
            in_specs=[once] * pairs + [right_spec, right_once, right_once] + [once] * len(others),
            out_specs=[whole] * 4,
            scratch_shapes=[pltpu.VMEM((tasks, rows, width), FLOAT)],
        ),
        out_shape=[out] * 4,
        compiler_params=pltpu.CompilerParams(vmem_limit_bytes=58 * MIB),
        cost_estimate=CHEAP,
    )(place, *lefts, *rights, *others)
    return [(sent0, kept0), (sent1, kept1)]


BLOCK = 128


def distinct_kernel(rows_owner, owners, round_ref, ids_ref, rank_ref, slot_ref, wanted_ref, held, total):
    count = ids_ref.shape[1]
    slots = wanted_ref.shape[1] // owners
    blocks = count // BLOCK

    def down(row):
        return jnp.broadcast_to(row, (BLOCK, BLOCK)).T

    def fold(tile):
        return jnp.sum(tile.reshape(BLOCK // 8, 8, BLOCK), axis=0)

    def sweep(term, targets, *rows):
        total[...] = jnp.zeros_like(total)

        def step(k, carry):
            start = pl.multiple_of(k * BLOCK, BLOCK)
            columns = [down(row[:, pl.ds(start, BLOCK)]) for row in rows]
            for block in range(targets):
                lanes = slice(block * BLOCK, (block + 1) * BLOCK)
                total[:, lanes] = total[:, lanes] + fold(term(columns, start, lanes))
            return carry

        lax.fori_loop(0, blocks, step, 0)
        return jnp.sum(total[...], axis=0, keepdims=True)

    place = lax.broadcasted_iota(jnp.int32, (BLOCK, BLOCK), 0) - lax.broadcasted_iota(
        jnp.int32, (BLOCK, BLOCK), 1
    )
    ids = ids_ref[...]

    total[...] = jnp.zeros_like(total)

    def earlier(k, carry):
        lanes = pl.ds(pl.multiple_of(k * BLOCK, BLOCK), BLOCK)
        column = down(ids_ref[:, lanes])
        same = (column == ids_ref[:, lanes]) & (place < 0)
        total[:, lanes] = total[:, lanes] + fold(jnp.where(same, 1.0, 0.0))

        def later(j, carry):
            lanes = pl.ds(pl.multiple_of(j * BLOCK, BLOCK), BLOCK)
            total[:, lanes] = total[:, lanes] + fold(jnp.where(column == ids_ref[:, lanes], 1.0, 0.0))
            return carry

        return lax.fori_loop(k + 1, blocks, later, carry)

    lax.fori_loop(0, blocks, earlier, 0)
    first = jnp.sum(total[...], axis=0, keepdims=True) == 0.0
    far = float(owners * rows_owner)
    held[0:1] = jnp.where(first, ids, far)

    def below(columns, start, lanes):
        return jnp.where(columns[0] < ids_ref[:, lanes], 1.0, 0.0)

    rank = sweep(below, blocks, held.at[0:1])
    owner = jnp.zeros_like(ids)
    start_before = jnp.zeros((1, 1), FLOAT)
    for index in range(1, owners):
        start_here = jnp.sum(
            jnp.where(held[0:1] < float(index * rows_owner), 1.0, 0.0), axis=1, keepdims=True
        )
        reached = ids >= float(index * rows_owner)
        owner = owner + jnp.where(reached, 1.0, 0.0)
        rank = rank - jnp.where(reached, start_here - start_before, 0.0)
        start_before = start_here
    rank_ref[...] = rank.astype(jnp.int32)
    turn = rank - (round_ref[0] * slots).astype(FLOAT)
    taken = (turn >= 0.0) & (turn < float(slots))
    slot = jnp.where(taken, owner * float(slots) + turn, -1.0)
    slot_ref[...] = slot.astype(jnp.int32)
    held[0:1] = jnp.where(first, slot, -1.0)
    held[1:2] = ids - owner * float(rows_owner) + 1.0

    lane = lax.broadcasted_iota(jnp.int32, (1, BLOCK), 1)

    def asked(columns, start, lanes):
        wanted = (lane + lanes.start).astype(FLOAT)
        return jnp.where(columns[0] == wanted, columns[1], 0.0)

    asked_count = wanted_ref.shape[1]
    summed = sweep(asked, asked_count // BLOCK, held.at[0:1], held.at[1:2])
    wanted_ref[...] = (summed[:, :asked_count] - 1.0).astype(jnp.int32)


def distinct(turn, ids, rows_owner, owners, slots):
    count = ids.shape[0]
    whole = pl.BlockSpec((1, count), lambda i, turn: (0, 0))
    asked = pl.BlockSpec((1, owners * slots), lambda i, turn: (0, 0))
    out = jax.ShapeDtypeStruct((1, count), jnp.int32)
    values = pl.pallas_call(
        functools.partial(distinct_kernel, rows_owner, owners),
        grid_spec=pltpu.PrefetchScalarGridSpec(
            num_scalar_prefetch=1,
            grid=(1,),
            in_specs=[whole],
            out_specs=[whole, whole, asked],
            scratch_shapes=[pltpu.VMEM((8, count), FLOAT), pltpu.VMEM((8, count), FLOAT)],
        ),
        out_shape=[out, out, jax.ShapeDtypeStruct((1, owners * slots), jnp.int32)],
        compiler_params=pltpu.CompilerParams(vmem_limit_bytes=32 * MIB),
        cost_estimate=pl.CostEstimate(flops=1, bytes_accessed=1, transcendentals=0),
    )(jnp.reshape(turn, (1,)).astype(jnp.int32), ids.astype(FLOAT).reshape(1, count))
    return [value.reshape(-1) for value in values]


def match_kernel(left_ref, right_ref, rows_ref, out_ref):
    hot = jnp.where(left_ref[...] == right_ref[...], 1.0, 0.0).astype(BFLOAT)
    out_ref[...] = matmul(hot, rows_ref[...]).astype(out_ref.dtype)


def match_pairs_kernel(right_ref, rows_ref, out_ref):
    count = out_ref.shape[0]
    left = 2 * (pl.program_id(0) * count + lax.broadcasted_iota(jnp.int32, (count, 1), 0))
    sums = []
    for odd in range(2):
        hot = jnp.where(left + odd == right_ref[...], 1.0, 0.0).astype(BFLOAT)
        sums.append(matmul(hot, rows_ref[...]))
    out_ref[...] = jnp.concatenate(sums, axis=1)


def match_pairs(stored, right, rows):
    count, width = rows.shape
    wide = next(b for b in (240, 120, 80, 40, 24, 16, 8) if stored[0] % b == 0)
    return pl.pallas_call(
        match_pairs_kernel,
        grid=(stored[0] // wide,),
        in_specs=[pl.BlockSpec((1, count), lambda i: (0, 0)), pl.BlockSpec((count, width), lambda i: (0, 0))],
        out_specs=pl.BlockSpec((wide, 2 * width), lambda i: (i, 0)),
        out_shape=jax.ShapeDtypeStruct(stored, FLOAT),
        compiler_params=pltpu.CompilerParams(vmem_limit_bytes=48 * MIB),
        cost_estimate=CHEAP,
    )(right.reshape(1, -1), rows)


def match_rows(left, right, rows, dtype):
    count, width = rows.shape
    wide = next(b for b in (512, 480, 256, 240, 128, 64, 32, 16) if left.shape[0] % b == 0)
    return pl.pallas_call(
        match_kernel,
        grid=(left.shape[0] // wide,),
        in_specs=[
            pl.BlockSpec((wide, 1), lambda i: (i, 0)),
            pl.BlockSpec((1, count), lambda i: (0, 0)),
            pl.BlockSpec((count, width), lambda i: (0, 0)),
        ],
        out_specs=pl.BlockSpec((wide, width), lambda i: (i, 0)),
        out_shape=jax.ShapeDtypeStruct((left.shape[0], width), dtype),
        compiler_params=pltpu.CompilerParams(vmem_limit_bytes=48 * MIB),
        cost_estimate=pl.CostEstimate(flops=1, bytes_accessed=1, transcendentals=0),
    )(left.reshape(-1, 1), right.reshape(1, -1), rows)


def swap(value, axis, bit):
    size = lax.axis_size(axis)
    return lax.ppermute(value, axis, [(i, i ^ bit) for i in range(size)])


def hop(value, bit):
    return swap(value, "mp", 2) if bit == X_BIT else swap(value, "dp", bit)


def first_hop(pieces, orders):
    return [(keep, hop(send, order[0])) for (send, keep), order in zip(pieces, orders)]


def next_sums_kernel(own_ref, came_ref, own_far_ref, came_far_ref, keep_ref, send_ref):
    keep_ref[...] = own_ref[...].astype(FLOAT) + came_ref[...].astype(FLOAT)
    send_ref[...] = (own_far_ref[...].astype(FLOAT) + came_far_ref[...].astype(FLOAT)).astype(BFLOAT)


def next_sums(state):
    own, came = state
    shape = own.shape
    half = shape[0] // 2
    near = pl.BlockSpec((1,) + shape[1:], lambda i: (i, 0, 0, 0))
    far = pl.BlockSpec((1,) + shape[1:], lambda i: (i + half, 0, 0, 0))
    return pl.pallas_call(
        next_sums_kernel,
        grid=(half,),
        in_specs=[near, near, far, far],
        out_specs=[near, near],
        out_shape=[jax.ShapeDtypeStruct((half,) + shape[1:], kind) for kind in (FLOAT, BFLOAT)],
        cost_estimate=CHEAP,
    )(own, came, own, came)


class Reduction:
    def __init__(self):
        self.states, self.orders, self.done, self.last = {}, {}, {}, None

    def begin(self, group, pieces, orders):
        for half, ((send, keep), order) in enumerate(zip(pieces, orders)):
            self.states[group, half] = (keep, hop(send, order[0]))
            self.orders[group, half] = order
            self.done[group, half] = 1

    def tie(self, key, value):
        own, came = self.states[key]
        own, value = lax.optimization_barrier((own, value))
        self.states[key] = (own, came)
        return value

    def advance(self, *keys):
        for key in keys:
            own, came = self.states[key]
            if self.last is not None and self.last != key:
                own = self.tie(self.last, own)
            keep, send = next_sums((own, came))
            self.states[key] = (keep, hop(send, self.orders[key][self.done[key]]))
            self.done[key] += 1
            self.last = key

    def complete(self, group):
        keys = [(group, 0), (group, 1)]
        for key in keys:
            while self.done[key] < len(self.orders[key]):
                self.advance(key)
        return finish_group([self.states[key] for key in keys])


def part_of(rows):
    return -(-rows // 32) * 8


def store_halves(side, keep_ref, send_ref, value):
    half = keep_ref.shape[0]
    for index in range(2):
        piece = value[index * half : (index + 1) * half]

        @pl.when(side == index)
        def _():
            keep_ref[...] = piece

        @pl.when(side != index)
        def _():
            send_ref[...] = piece


def collect_kernel(place_ref, tables_ref, zero_ref, one_ref, two_ref, inner_ref, mixed_ref, keep_ref, send_ref, rows_ref):
    groups, examples, _, width = inner_ref.shape
    length = tables_ref.shape[0]
    column = width // 4

    def summed(ref, row):
        return sum(ref[e, row : row + 1] for e in range(examples))

    def natural(ref, block):
        parts = []
        for group in range(groups):
            step = place_ref[group]
            row = sum(ref[step, e, 0:1] for e in range(examples))
            parts.append(row[:, block * column : (block + 1) * column])
        return jnp.concatenate(parts, axis=1)

    rows_ref[length:] = jnp.zeros((rows_ref.shape[0] - length, rows_ref.shape[1]), FLOAT)
    rows_ref[:length] = tables_ref[...]
    rows = [summed(zero_ref, 2), summed(zero_ref, 3), summed(zero_ref, 0), summed(zero_ref, 1)]
    rows += [natural(mixed_ref, 0), natural(mixed_ref, 2), summed(one_ref, 2), summed(one_ref, 0), summed(one_ref, 1)]
    rows += [natural(inner_ref, block) for block in range(4)]
    rows += [summed(two_ref, 2), summed(two_ref, 0), summed(two_ref, 1)]
    for index, row in enumerate(rows):
        rows_ref[length + index : length + index + 1] = row
    first = length + len(rows)
    for example in range(examples):
        task = place_ref[groups + example]
        at = pl.ds(first + task, 1)
        rows_ref[at] = rows_ref[at] + two_ref[example, 3:4]
    store_halves(place_ref[groups + examples], keep_ref, send_ref, rows_ref)


def collect(place, tables, zero, one, two, inner, mixed, rows):
    half = jax.ShapeDtypeStruct((2 * part_of(rows), tables.shape[1]), FLOAT)
    return pl.pallas_call(
        collect_kernel,
        grid_spec=pltpu.PrefetchScalarGridSpec(
            num_scalar_prefetch=1,
            grid=(1,),
            in_specs=[
                pl.BlockSpec(v.shape, lambda i, p, d=len(v.shape): (0,) * d)
                for v in (tables, zero, one, two, inner, mixed)
            ],
            out_specs=[pl.BlockSpec(half.shape, lambda i, p: (0, 0))] * 2,
            scratch_shapes=[pltpu.VMEM((2 * half.shape[0], half.shape[1]), FLOAT)],
        ),
        out_shape=[half, half],
        compiler_params=pltpu.CompilerParams(vmem_limit_bytes=32 * MIB),
        cost_estimate=CHEAP,
    )(place, tables, zero, one, two, inner, mixed)


def small_call(body, side, values, outputs):
    def whole(value):
        return pl.BlockSpec(value.shape, lambda i, p, d=len(value.shape): (0,) * d)

    return pl.pallas_call(
        body,
        grid_spec=pltpu.PrefetchScalarGridSpec(
            num_scalar_prefetch=1,
            grid=(1,),
            in_specs=[whole(v) for v in values],
            out_specs=[whole(v) for v in outputs],
        ),
        out_shape=outputs,
        compiler_params=pltpu.CompilerParams(vmem_limit_bytes=32 * MIB),
        cost_estimate=CHEAP,
    )(jnp.reshape(side, (1,)).astype(jnp.int32), *values)


def add_rows_kernel(side_ref, own_ref, came_ref, keep_ref, send_ref):
    store_halves(side_ref[0], keep_ref, send_ref, own_ref[...] + came_ref[...])


def add_columns_kernel(side_ref, own_ref, came_ref, keep_ref, send_ref):
    total = own_ref[...] + came_ref[...]
    width = keep_ref.shape[2]
    for index in range(2 * keep_ref.shape[0]):
        piece = total[:, index * width : (index + 1) * width]

        @pl.when(side_ref[0] == index % 2)
        def _():
            keep_ref[index // 2] = piece

        @pl.when(side_ref[0] != index % 2)
        def _():
            send_ref[index // 2] = piece


def add_blocks_kernel(side_ref, own_ref, came_ref, keep_ref, send_ref):
    for index in range(2 * keep_ref.shape[0]):
        piece = own_ref[index] + came_ref[index]

        @pl.when(side_ref[0] == index % 2)
        def _():
            keep_ref[index // 2] = piece

        @pl.when(side_ref[0] != index % 2)
        def _():
            send_ref[index // 2] = piece


def add_last_kernel(side_ref, own_ref, came_ref, out_ref):
    out_ref[...] = own_ref[0] + came_ref[0]


def join_kernel(side_ref, own_ref, came_ref, out_ref):
    half = own_ref.shape[0]
    for index in range(2):
        rows = slice(index * half, (index + 1) * half)

        @pl.when(side_ref[0] == index)
        def _():
            out_ref[rows] = own_ref[...]

        @pl.when(side_ref[0] != index)
        def _():
            out_ref[rows] = came_ref[...]


def embed_kernel(words_ref, tables_ref, segment_ref, scale_ref, embedded_ref, normed_ref, low_ref):
    length = embedded_ref.shape[1]
    words = jnp.concatenate([words_ref[m, 0] for m in range(words_ref.shape[0])], axis=1).astype(FLOAT)
    part = jnp.where(segment_ref[0] == 1, tables_ref[length + 1 : length + 2], tables_ref[length : length + 1])
    embedded = words + tables_ref[:length] + part
    embedded_ref[0] = embedded
    normed = layer_norm(embedded, scale_ref[0:1], scale_ref[1:2])
    normed_ref[0] = normed
    low_ref[0] = normed.astype(BFLOAT)


def embed(words, table_rows, segments, scales):
    groups, examples, length, width = words.shape
    full = groups * width
    rows = pl.BlockSpec((1, length, full), lambda e: (e, 0, 0))
    return pl.pallas_call(
        embed_kernel,
        cost_estimate=CHEAP,
        grid=(examples,),
        in_specs=[
            pl.BlockSpec((groups, 1, length, width), lambda e: (0, e, 0, 0)),
            pl.BlockSpec(table_rows.shape, lambda e: (0, 0)),
            pl.BlockSpec((1, length, 1), lambda e: (e, 0, 0)),
            pl.BlockSpec(scales.shape, lambda e: (0, 0)),
        ],
        out_specs=[rows, rows, rows],
        out_shape=[
            jax.ShapeDtypeStruct((examples, length, full), kind) for kind in (FLOAT, FLOAT, BFLOAT)
        ],
        compiler_params=pltpu.CompilerParams(vmem_limit_bytes=48 * MIB),
    )(words, table_rows, segments[:, :, None], scales)


LANES = 128


def finish_group_kernel(own0_ref, came0_ref, own1_ref, came1_ref, total_ref, gram_ref):
    tasks = own0_ref.shape[1]
    half = own0_ref.shape[3]
    for task in range(tasks):
        total_ref[task, :, :half] = own0_ref[0, task] + came0_ref[0, task].astype(FLOAT)
        total_ref[task, :, half:] = own1_ref[0, task] + came1_ref[0, task].astype(FLOAT)
    lane = lax.broadcasted_iota(jnp.int32, gram_ref.shape, 1)
    gram = jnp.zeros(gram_ref.shape, FLOAT)
    for i in range(tasks):
        for j in range(i, tasks):
            product = jnp.sum(total_ref[i] * total_ref[j], axis=0, keepdims=True)
            product = jnp.sum(product, axis=1, keepdims=True)
            gram = gram + jnp.where((lane == i * tasks + j) | (lane == j * tasks + i), product, 0.0)
    gram_ref[...] = gram


def finish_group(states):
    _, tasks, rows, half = states[0][0].shape
    return pl.pallas_call(
        finish_group_kernel,
        out_shape=[
            jax.ShapeDtypeStruct((tasks, rows, 2 * half), FLOAT),
            jax.ShapeDtypeStruct((1, LANES), FLOAT),
        ],
        compiler_params=pltpu.CompilerParams(vmem_limit_bytes=32 * MIB),
        cost_estimate=CHEAP,
    )(*states[0], *states[1])


def adam_update(weight, gradient, first_moment, second_moment, step_rate, weight_decay):
    moment_new = BETA_ONE * first_moment + (1.0 - BETA_ONE) * gradient
    square_new = BETA_TWO * second_moment + (1.0 - BETA_TWO) * gradient * gradient
    corrected = moment_new / (1.0 - BETA_ONE**STEP)
    scaled = square_new / (1.0 - BETA_TWO**STEP)
    weight_new = weight - step_rate * (
        corrected / (jnp.sqrt(scaled) + ADAM_EPS) + weight_decay * weight
    )
    return (moment_new, square_new, weight_new)


def update_kernel(sizes, order_ref, scalar_ref, count_ref, *refs):
    tasks, tables_end, vectors_end = sizes
    small_ref, word_grad_ref, *refs = refs
    groups, refs = refs[:3], refs[3:]
    inputs, outputs, report_ref = refs[:15], refs[15:35], refs[35]
    step = pl.program_id(0)

    def scalar(ref, index):
        return jnp.full((1, 1), ref[0, index], FLOAT)

    gram = [[scalar(scalar_ref, i * tasks + j) for j in range(tasks)] for i in range(tasks)]
    mix = [jnp.zeros((1, 1), FLOAT)] * tasks
    for first in range(tasks):
        current = [jnp.full((1, 1), float(k == first), FLOAT) for k in range(tasks)]
        for position in range(tasks):
            other = order_ref[0, position]
            row = [scalar(scalar_ref, other * tasks + k) for k in range(tasks)]
            dot = sum(current[k] * row[k] for k in range(tasks))
            square = scalar(scalar_ref, other * tasks + other)
            factor = jnp.where(other == first, 0.0, jnp.minimum(dot, 0.0) / square)
            current = [current[k] - jnp.where(other == k, factor, 0.0) for k in range(tasks)]
        mix = [mix[k] + current[k] for k in range(tasks)]
    squares = scalar(scalar_ref, tasks * tasks)
    for i in range(tasks):
        for j in range(tasks):
            squares = squares + mix[i] * mix[j] * gram[i][j]
    norm = jnp.sqrt(squares)
    scale = jnp.minimum(1.0, CLIP / norm)
    loss = sum(scalar(scalar_ref, tasks * tasks + 1 + t) / scalar(count_ref, t) for t in range(tasks))
    lane = lax.broadcasted_iota(jnp.int32, report_ref.shape, 1)
    report_ref[...] = jnp.where(lane == 0, norm, loss)

    def update(index, gradient, rate, decay):
        weight_ref, first_ref, second_ref = inputs[3 * index : 3 * index + 3]
        clipped = gradient * scale
        values = adam_update(weight_ref[...], clipped, first_ref[...], second_ref[...], rate, decay)
        for out_ref, value in zip(outputs[4 * index : 4 * index + 4], (clipped, *values)):
            out_ref[...] = value

    update(0, word_grad_ref[...], RATE_WEIGHT, DECAY)
    for group, group_ref in enumerate(groups):

        @pl.when(step == group)
        def _():
            update(2, sum(mix[t] * group_ref[t] for t in range(tasks)), RATE_WEIGHT, DECAY)

    @pl.when(step == 0)
    def _():
        update(1, small_ref[:tables_end], RATE_WEIGHT, DECAY)
        update(3, small_ref[tables_end:vectors_end], RATE_VECTOR, 0.0)
        update(4, small_ref[vectors_end : vectors_end + tasks], RATE_WEIGHT, DECAY)


def update_all(order, scalars, counts, small, word_grad, groups, arrays):
    steps = len(groups)
    tasks = groups[0].shape[0]
    tables_end = arrays[3].shape[0]

    def whole(value):
        return pl.BlockSpec(value.shape, lambda i, d=len(value.shape): (0,) * d)

    def spec(index, value):
        rows, width = value.shape
        if index == 0:
            return pl.BlockSpec((rows // steps, width), lambda i: (i, 0))
        if index == 2:
            return pl.BlockSpec((rows, width // steps), lambda i: (0, i))
        return whole(value)

    scalar_spec = pl.BlockSpec(memory_space=pltpu.SMEM)
    report = jax.ShapeDtypeStruct((8, LANES), FLOAT)
    outputs = [(index, arrays[3 * index]) for index in range(5) for _ in range(4)]
    return pl.pallas_call(
        functools.partial(update_kernel, (tasks, tables_end, tables_end + arrays[9].shape[0])),
        grid=(steps,),
        in_specs=[scalar_spec] * 3
        + [whole(small), spec(0, word_grad)]
        + [whole(group) for group in groups]
        + [spec(i // 3, value) for i, value in enumerate(arrays)],
        out_specs=[spec(index, value) for index, value in outputs] + [whole(report)],
        out_shape=[jax.ShapeDtypeStruct(value.shape, FLOAT) for _, value in outputs] + [report],
        compiler_params=pltpu.CompilerParams(vmem_limit_bytes=56 * MIB),
    )(order.reshape(1, -1), scalars, counts.reshape(1, -1), small, word_grad, *groups, *arrays)


def on_device(
    token_ids,
    segment_ids,
    task_ids,
    task_order,
    counted,
    targets,
    word_table,
    word_first,
    word_second,
    tables,
    tables_first,
    tables_second,
    matrices,
    matrices_first,
    matrices_second,
    vectors,
    vectors_first,
    vectors_second,
    regressor,
    regressor_first,
    regressor_second,
):
    word_stored = word_table.shape
    nd = lax.axis_size("dp")
    nm = lax.axis_size("mp")
    m_index = lax.axis_index("mp")
    rows_own, width_all = matrices.shape
    width_own = width_all // 12
    full = rows_own * nd
    quarter = 4 * width_own
    tasks = regressor.shape[0]
    slice_width = tables.shape[1]
    batch, length = token_ids.shape
    own = batch // nm
    tokens = own * length

    def mine(rows):
        return lax.dynamic_slice_in_dim(rows, m_index * own, own, 0)

    rows_owner = word_stored[0] * word_stored[1] // width_own
    token_flat = token_ids.reshape(-1)
    slots = token_flat.shape[0] * 5 // 8 // nd
    task_all_hot = (task_ids[:, None] == jnp.arange(tasks, dtype=jnp.int32)[None, :]).astype(FLOAT)
    counted_all = counted.astype(FLOAT)
    counts_here = jnp.sum(task_all_hot * jnp.sum(counted_all, axis=1)[:, None], axis=0)
    high = jnp.floor(counts_here / 256.0)
    coded = jnp.concatenate([high, counts_here - 256.0 * high])
    coded = jnp.pad(coded, (0, slice_width - coded.shape[0]))[None]
    small = jnp.concatenate([tables, vectors, regressor, coded]).astype(BFLOAT)
    small_all = lax.all_to_all(jnp.broadcast_to(small, (nd, *small.shape)), "dp", 0, 0, tiled=True)
    rank, slot, wanted = distinct(jnp.int32(0), token_flat, rows_owner, nd, slots)

    def exchange(rows):
        return lax.all_to_all(rows.reshape(nd, slots, *rows.shape[1:]), "dp", 0, 0, tiled=True).reshape(rows.shape)

    largest = jnp.broadcast_to(jnp.max(rank), (nd, 1))
    asked = jnp.concatenate([wanted.reshape(nd, slots), largest], axis=1)
    asked, small_all = lax.optimization_barrier((asked, small_all))
    asked = lax.all_to_all(asked, "dp", 0, 0, tiled=True)
    rounds = jnp.max(asked[:, slots]) // slots + 1
    asked = asked[:, :slots].reshape(-1)
    coded_all = small_all[:, -1].astype(FLOAT)
    small_all = small_all[:, :-1].transpose(1, 0, 2).reshape(-1, full)
    task_counts = jnp.sum(256.0 * coded_all[:, :tasks] + coded_all[:, tasks : 2 * tasks], axis=0)
    words_low = word_table.astype(BFLOAT).reshape(-1, width_own)
    matrices_low = matrices.astype(BFLOAT)

    def gather_block(start, stop):
        part = matrices_low[:, start * quarter : stop * quarter]
        return lax.all_gather(part, ("mp", "dp"), axis=0, tiled=True).reshape(nm, full, -1)

    block_a, block_uv = gather_block(0, 1), gather_block(1, 3)
    small_full = small_all.astype(FLOAT)
    table_full = small_full[: length + 2]
    vector_full = small_full[length + 2 : length + 2 + vectors.shape[0]]
    regressor_full = small_full[length + 2 + vectors.shape[0] :]
    masks = (3, 1, 2, 0)
    order = jnp.stack([jnp.bitwise_xor(m_index, mask) for mask in masks])
    place_of = jnp.stack([jnp.bitwise_xor(m_index, m) for m in range(nm)])
    place_of = jnp.take(jnp.array([masks.index(k) for k in range(nm)], jnp.int32), place_of)

    def columns(rows):
        return rows.reshape(-1, nm, width_own).transpose(1, 0, 2).reshape(nm, 1, -1)

    blank = jnp.zeros_like(vector_full[2])
    projection_bias = columns(jnp.stack([vector_full[2], blank, vector_full[3], blank]))
    up_bias = columns(vector_full[7:11])

    task_own = mine(task_ids)
    task_hot = mine(task_all_hot)
    segment_own = mine(segment_ids)
    counted_own = mine(counted_all)
    targets_own = mine(targets)

    owner_rows = jnp.arange(rows_owner, dtype=jnp.int32)
    slot_rows = jnp.arange(nd * slots, dtype=jnp.int32)

    def look_up(slot_now, asked_now):
        came = exchange(match_rows(asked_now, owner_rows, words_low, BFLOAT))
        return match_rows(slot_now, slot_rows, came, BFLOAT)

    def look_up_round(state):
        turn, found = state
        _, slot_now, wanted_now = distinct(turn, token_flat, rows_owner, nd, slots)
        return turn + 1, found + look_up(slot_now, exchange(wanted_now))

    looked = look_up(slot, asked)
    looked = lax.while_loop(lambda state: state[0] < rounds, look_up_round, (jnp.int32(1), looked))[1]
    swapped = lax.all_to_all(looked.reshape(nm, tokens, width_own), "mp", 0, 0, tiled=True)
    embedded, hidden_zero, zero_low = embed(
        swapped.reshape(nm, own, length, width_own), table_full, segment_own, vector_full[0:2]
    )

    rows_type = jax.ShapeDtypeStruct((own, length, full), FLOAT)
    group_low = jax.ShapeDtypeStruct((nm, own, length, quarter), BFLOAT)
    group_type = jax.ShapeDtypeStruct((nm, own, length, quarter), FLOAT)
    half_low = jax.ShapeDtypeStruct((nm // 2, own, length, quarter), BFLOAT)
    rows_low = jax.ShapeDtypeStruct(rows_type.shape, BFLOAT)
    sums_type = jax.ShapeDtypeStruct((own, 8, full), FLOAT)
    step_sums = jax.ShapeDtypeStruct((nm, own, 8, quarter), FLOAT)
    row_scratch = pltpu.VMEM((length, full), FLOAT)
    saved, attended = over_groups(
        attention_forward_kernel,
        order,
        [("rows", zero_low), ("group", block_a), ("group", projection_bias)],
        [("steps", group_low), ("rows", rows_type)],
    )
    regressor_rows = jnp.dot(task_hot, regressor_full, precision=HIGHEST)
    error_scale = 2.0 / jnp.dot(task_hot, task_counts, precision=HIGHEST)
    heads = jnp.stack([regressor_rows, jnp.broadcast_to(error_scale[:, None], regressor_rows.shape)], axis=1)
    active_other, active_far, active_own, slope, residual_one, one_low, grad_two, grad_fed, two_sums = over_groups(
        feed_forward_kernel,
        order,
        [
            ("rows", hidden_zero), ("rows", attended), ("group left", block_uv), ("group right", block_uv),
            ("group", up_bias), ("whole", vector_full), ("rows", heads),
            ("rows", jnp.stack([targets_own, counted_own], axis=-1)),
        ],
        [
            ("rows", rows_low), ("rows", rows_low), ("last", half_low), ("steps", group_type), ("rows", rows_type),
            ("rows", rows_low), ("rows", rows_type), ("rows", rows_low), ("rows", sums_type),
        ],
        [row_scratch, row_scratch],
    )
    local_errors = jnp.sum(task_hot * two_sums[:, 4, 0:1], axis=0)

    d_index = lax.axis_index("dp")
    task_near = lax.dynamic_slice_in_dim(task_ids, jnp.bitwise_xor(m_index, 1) * own, own, 0)
    task_chip = jnp.concatenate([task_own, task_near])
    place = jnp.concatenate([task_chip, jnp.stack([d_index])]).astype(jnp.int32)

    def near(value):
        return swap(value, "mp", 1)

    z_bits = tuple(1 << k for k in range(1, nd.bit_length() - 1))
    early = ((X_BIT, 1) + z_bits, (1, X_BIT) + z_bits)
    late = ((X_BIT, 1) + z_bits, z_bits + (1, X_BIT))
    inner_other, inner_far, inner_own, inner_sums, grad_one, grad_attended, one_sums = over_groups(
        feed_backward_kernel,
        order,
        [
            ("rows", grad_fed), ("steps", slope), ("group left", block_uv), ("group right", block_uv),
            ("rows", grad_two), ("rows", residual_one), ("whole", vector_full),
        ],
        [
            ("rows", rows_low), ("rows", rows_low), ("last", half_low), ("steps", step_sums), ("rows", rows_type),
            ("rows", rows_low), ("rows", sums_type),
        ],
        [row_scratch],
    )
    down_pieces = task_outer(
        place, [grad_fed, near(grad_fed)], [active_own, near(active_other), near(active_far)], tasks, nd, early
    )
    reduction = Reduction()
    reduction.begin("down", down_pieces, early)
    inner_own, down_pieces = lax.optimization_barrier((inner_own, down_pieces))
    up_pieces = task_outer(
        place, [one_low, near(one_low)], [inner_own, near(inner_other), near(inner_far)], tasks, nd, late
    )
    reduction.begin("up", up_pieces, late)
    grad_attended, up_pieces = lax.optimization_barrier((grad_attended, up_pieces))
    mixed_other, mixed_far, mixed_own, mixed_sums, word_rows, table_sums, zero_sums = over_groups(
        attention_backward_kernel,
        order,
        [
            ("steps", saved), ("group", block_a), ("rows", grad_attended), ("rows", grad_one),
            ("rows", embedded), ("rows", segment_own[:, :, None]), ("whole", vector_full),
        ],
        [
            ("rows", rows_low), ("rows", rows_low), ("last", half_low), ("steps", step_sums),
            ("words", jax.ShapeDtypeStruct((nm, own, length, width_own), BFLOAT)),
            ("whole", jax.ShapeDtypeStruct((length, full), FLOAT)), ("rows", sums_type),
        ],
        [row_scratch],
    )
    mixed_own, word_rows = reduction.tie(("down", 0), (mixed_own, word_rows))
    reduction.advance(("down", 0), ("down", 1), ("up", 1))
    mixed_own = reduction.tie(("up", 1), mixed_own)
    up_half = reduction.states["up", 0]
    mixed_own, up_half = lax.optimization_barrier((mixed_own, up_half))
    reduction.states["up", 0] = up_half
    attention_pieces = task_outer(
        place,
        [zero_low, near(zero_low)],
        [mixed_own, near(mixed_other), near(mixed_far)],
        tasks,
        nd,
        early,
        others=[grad_attended, near(grad_attended)],
    )
    reduction.begin("attention", attention_pieces, early)
    kept = reduction.tie(("up", 0), attention_pieces[0][1])
    reduction.states["attention", 0] = (kept, reduction.states["attention", 0][1])
    reduction.advance(("up", 0), ("down", 0), ("down", 1))
    word_rows = reduction.tie(("down", 1), word_rows)
    reduction.advance(("up", 1), ("down", 0), ("down", 1))

    word_rows = lax.all_to_all(word_rows.reshape(nm, tokens, width_own), "mp", 0, 0, tiled=True)
    word_rows = word_rows.reshape(nm * tokens, width_own)
    word_rows = reduction.tie(reduction.last, word_rows)

    def give_back(slot_now, asked_now, sums):
        return match_pairs(word_stored, asked_now, exchange(sums))

    def give_back_round(state):
        turn, given = state
        _, slot_now, wanted_now = distinct(turn, token_flat, rows_owner, nd, slots)
        return turn + 1, given + give_back(
            slot_now, exchange(wanted_now), match_rows(slot_rows, slot_now, word_rows, BFLOAT)
        )

    slot_sums = match_rows(slot_rows, slot, word_rows, BFLOAT)
    slot_sums, table_sums, zero_sums, one_sums, inner_sums, mixed_sums, two_sums = lax.optimization_barrier(
        (slot_sums, table_sums, zero_sums, one_sums, inner_sums, mixed_sums, two_sums)
    )
    slot_sums = reduction.tie(reduction.last, slot_sums)
    word_grad = give_back(slot, asked, slot_sums)
    word_grad = lax.while_loop(lambda state: state[0] < rounds, give_back_round, (jnp.int32(1), word_grad))[1]

    small_rows = length + 2 + vectors.shape[0] + tasks
    rows_part = part_of(small_rows)
    core, x_index = m_index % 2, (m_index // 2) % 2
    collect_place = jnp.concatenate([place_of, task_own, jnp.stack([core])]).astype(jnp.int32)
    keep, send = collect(
        collect_place, table_sums, zero_sums, one_sums, two_sums, inner_sums, mixed_sums, small_rows
    )

    def tied(value):
        return reduction.tie(reduction.last, value)

    came = swap(send, "mp", 1)
    reduction.advance(("attention", 0), ("attention", 1))
    part = jax.ShapeDtypeStruct((rows_part, full), FLOAT)
    keep, send = small_call(add_rows_kernel, x_index, [tied(keep), came], [part, part])
    came = swap(send, "mp", 2)
    reduction.advance(("up", 0), ("up", 1))
    finished = {"down": reduction.complete("down")}
    part = jax.ShapeDtypeStruct((nd // 2, rows_part, slice_width), FLOAT)
    keep, send = small_call(add_columns_kernel, d_index % 2, [tied(keep), came], [part, part])
    came = swap(send, "dp", 1)
    reduction.advance(("attention", 0), ("attention", 1))
    for index, bit in enumerate(z_bits):
        if index == len(z_bits) - 1:
            reduction.advance(("up", 0))
            word_grad = tied(word_grad)
        part = jax.ShapeDtypeStruct((keep.shape[0] // 2, rows_part, slice_width), FLOAT)
        keep, send = small_call(add_blocks_kernel, (d_index // bit) % 2, [tied(keep), came], [part, part])
        came = swap(send, "dp", bit)
    finished["up"] = reduction.complete("up")
    reduction.advance(("attention", 0), ("attention", 1))
    part = jax.ShapeDtypeStruct((rows_part, slice_width), FLOAT)
    (small_grad,) = small_call(add_last_kernel, core, [tied(keep), came], [part])
    came = swap(small_grad, "mp", 2)
    part = jax.ShapeDtypeStruct((2 * rows_part, slice_width), FLOAT)
    (small_grad,) = small_call(join_kernel, x_index, [small_grad, came], [part])
    came = swap(small_grad, "mp", 1)
    part = jax.ShapeDtypeStruct((4 * rows_part, slice_width), FLOAT)
    (small_grad,) = small_call(join_kernel, core, [small_grad, came], [part])
    finished["attention"] = reduction.complete("attention")
    groups, grams = [list(values) for values in zip(*[finished[k] for k in ("attention", "up", "down")])]
    local_squares = jnp.sum(word_grad * word_grad) + jnp.sum(small_grad * small_grad) / nm
    local = jnp.concatenate([jnp.reshape(local_squares, (1,)), local_errors])
    scalars = sum(grams) + jnp.pad(local, (tasks * tasks, LANES - tasks * tasks - local.shape[0]))[None]
    for axis in ("mp", "dp"):
        bit = 1
        while bit < lax.axis_size(axis):
            scalars = scalars + swap(scalars, axis, bit)
            bit *= 2
    *updated, report = update_all(
        task_order, scalars, task_counts, small_grad, word_grad, groups,
        [
            word_table, word_first, word_second, tables, tables_first, tables_second,
            matrices, matrices_first, matrices_second, vectors, vectors_first, vectors_second,
            regressor, regressor_first, regressor_second,
        ],
    )
    return (*updated, report[0, 0], report[0, 1], task_counts)


def solution(mesh):
    placed = (
        P("dp", None),
        P("dp", None),
        P("dp"),
        P(),
        P("dp", None),
        P("dp", None),
        P("dp", "mp"),
        P("dp", "mp"),
        P("dp", "mp"),
        P(None, "dp"),
        P(None, "dp"),
        P(None, "dp"),
        P("dp", "mp"),
        P("dp", "mp"),
        P("dp", "mp"),
        P(None, "dp"),
        P(None, "dp"),
        P(None, "dp"),
        P(None, "dp"),
        P(None, "dp"),
        P(None, "dp"),
    )
    return jax.shard_map(
        on_device,
        mesh=mesh,
        in_specs=placed,
        out_specs=(
            P("dp", "mp"),
            P("dp", "mp"),
            P("dp", "mp"),
            P("dp", "mp"),
            P(None, "dp"),
            P(None, "dp"),
            P(None, "dp"),
            P(None, "dp"),
            P("dp", "mp"),
            P("dp", "mp"),
            P("dp", "mp"),
            P("dp", "mp"),
            P(None, "dp"),
            P(None, "dp"),
            P(None, "dp"),
            P(None, "dp"),
            P(None, "dp"),
            P(None, "dp"),
            P(None, "dp"),
            P(None, "dp"),
            P(),
            P(),
            P(),
        ),
        check_vma=False,
    )
```

time: 3040 us -> 702 us (0.23)
  waiting for transfers between devices: 1710 us -> 190 us
  blocking collectives: 433 us -> 0 us
  other arithmetic: 349 us -> 16.5 us
  Pallas kernels: 0 us -> 332 us
  matrix products: 230 us -> 0.28 us
  local copies, waits for them, and re-layouts: 243 us -> 64.5 us
  starting transfers between devices: 1.22 us -> 69.6 us
  between operations: 60.4 us -> 18.6 us
    psum x5 -> x0, waiting for transfers between devices: 662 us -> none  [the longest x2 409 us: mixed_sum(): return lax.psum(partial_value, 'mp')]
    reduce_scatter x1 -> x0, waiting for transfers between devices: 487 us -> none  [on_device(): lax.psum_scatter(dense_words, 'dp', scatter_dimension=0, tiled=True)]
    psum x9 -> x0, blocking collectives: 346 us -> none  [the longest x7 283 us: on_device(): inner_dot = lax.psum(jnp.sum(current * other_grad), ('dp', 'mp'))]
    pallas_call x0 -> x43, Pallas kernels: none -> 332 us  [the longest x4 139 us: over_groups(): pl.pallas_call(body, grid_spec=pltpu.PrefetchScalarGridSpec(num_scalar_pr...]
    unnamed x11 -> x2, waiting for transfers between devices: 318 us -> 0.03 us
    all_gather x3 -> x2, waiting for transfers between devices: 246 us -> 0.01 us  [gather_block(): lax.all_gather(part, ('mp', 'dp'), axis=0, tiled=True).reshape(nm, full, -1)]
    dot_general x27 -> x2, matrix products: 230 us -> 0.28 us  [the longest x1 0.16 us: on_device(): regressor_rows = jnp.dot(task_hot, regressor_full, precision=HIGHEST)]
    reduce_sum x33 -> x6, other arithmetic: 174 us -> 4.93 us  [the longest x1 3.2 us: on_device(): jnp.sum(word_grad * word_grad) + jnp.sum(small_grad * small_grad) / nm]
  transfers between devices with their start and end apart: 10 -> 54, of which waited for: 8 -> 19; matrix products, arithmetic and copies ran while one was open for 14% -> 8% of each run, Pallas kernels for 0% -> 41%
where the time goes in v1:
time: 702 us; the launch traced here: 692 us
  Pallas kernels  332 us (47%)
  waiting for transfers between devices  190 us (27%)
  starting transfers between devices  69.6 us (10%)
  local copies, waits for them, and re-layouts  64.5 us (9%)
  between operations  18.6 us (3%)
  other arithmetic  16.5 us (2%)
    ppermute x46, waiting for transfers between devices, swap(): return lax.ppermute(value, axis, [(i, i ^ bit) for i in range(size)])  156 us
    pallas_call x4, Pallas kernels, over_groups(): pl.pallas_call(body, grid_spec=pltpu.PrefetchScalarGridSpec(num_scalar_pr...  139 us
    pallas_call x18, Pallas kernels, next_sums(): pl.pallas_call(next_sums_kernel, grid=(half,), in_specs=[near, near, far,...  59.5 us
    pallas_call x3, Pallas kernels, task_outer(): pl.pallas_call(functools.partial(task_outer_kernel, pairs, bool(others),...  49.4 us
    ppermute x46, starting transfers between devices, swap(): return lax.ppermute(value, axis, [(i, i ^ bit) for i in range(size)])  38.4 us
    pallas_call x1, Pallas kernels, distinct(): pl.pallas_call(functools.partial(distinct_kernel, rows_owner, owners), gr...  28.8 us
    all_to_all x2, waiting for transfers between devices, exchange(): lax.all_to_all(rows.reshape(nd, slots, *rows.shape[1:]), 'dp', 0, 0, tile...  25.7 us
    pallas_call x3, Pallas kernels, match_rows(): pl.pallas_call(match_kernel, grid=(left.shape[0] // wide,), in_specs=[pl....  22.2 us
  transfers between devices with their start and end apart: 54, of which 19 were waited for; matrix products, arithmetic and copies ran while one was open for 8% of the time, Pallas kernels for 41%

profile of v1, /device:TPU:0, one launch (start us, length us, event | category | flops | bytes accessed | tf_op | source)
XLA Modules:
  0.0 691.7 jit_solution(13285894715138421588)
XLA Ops:
  12.0 7.4 %all-to-all-start.4 = ((bf16[8,533,96]{1,2,0:T(8,128)(2,1)}), bf16[8,533,96]{1,2,0:T(8,128)(2,1)}, u32[]{:S(2)}, u32[]{:S(2)}) async-start(bf16[8,533,96]{1,2,0:T(8,128)(2,1)} %broadcast_in_dim.22), calls=%async_computation.4 | async-start | bytes 1966080 | tf_op jit(solution)/shard_map/all_to_all | solution.py:945
  19.5 28.8 %shard_map.389 = (s32[1,4096]{1,0:T(1,128)S(1)}, s32[1,4096]{1,0:T(1,128)S(1)}, s32[1,2560]{1,0:T(1,128)S(1)}) custom-call(s32[1]{0:T(128)} %constant.112.clone.1.round_ref, f32[1,4096]{1,0:T(1,128)S(1)} %bitcast.118), custom_call_target="tpu_custom_call" | custom-call | flops 1 | bytes 1 | tf_op jit(solution)/shard_map/pallas_call | solution.py:465
  50.4 6.0 all-to-all-start.5
  64.1 7.8 %shard_map.390 = bf16[2560,192]{1,0:T(8,128)(2,1)S(1)} custom-call(s32[2560,1]{1,0:T(8,128)S(1)} %reshape_reshape.16.left_ref, s32[1,3840]{1,0:T(1,128)S(1)} %iota.22.right_ref, bf16[3840,192]{1,0:T(8,128)(2,1)} %reshape.397.rows_ref), custom_call_target="tpu_custom_call" | custom-call | flops 1 | bytes 1 | tf_op jit(solution)/shard_map/pallas_call | solution.py:513
  73.4 4.6 all-to-all-start.6
  85.8 25.7 %all-to-all-done.6 = bf16[8,320,192]{1,2,0:T(8,128)(2,1)} async-done(((bf16[8,320,192]{1,2,0:T(8,128)(2,1)}), bf16[8,320,192]{1,2,0:T(8,128)(2,1)}, u32[]{:S(2)}, u32[]{:S(2)}) %all-to-all-start.6) | async-done | bytes 983072 | tf_op jit(solution)/shard_map/all_to_all | solution.py:949
  113.2 7.9 %shard_map.391 = bf16[4096,192]{1,0:T(8,128)(2,1)} custom-call(s32[4096,1]{1,0:T(8,128)S(1)} %copy.174.left_ref, s32[1,2560]{1,0:T(1,128)S(1)} %iota.21.right_ref, bf16[2560,192]{1,0:T(8,128)(2,1)S(1)} %bitcast.104), custom_call_target="tpu_custom_call" | custom-call | flops 1 | bytes 1 | tf_op jit(solution)/shard_map/pallas_call | solution.py:513
  143.0 7.3 %all-to-all-done.7 = bf16[4,1024,192]{1,2,0:T(8,128)(2,1)} async-done(((bf16[4,1024,192]{1,2,0:T(8,128)(2,1)}), bf16[4,1024,192]{1,2,0:T(8,128)(2,1)}, u32[]{:S(2)}, u32[]{:S(2)}) %all-to-all-start.7) | async-done | bytes 1572896 | tf_op jit(solution)/shard_map/all_to_all | solution.py:1004
  159.1 27.4 %shard_map.393 = (bf16[4,2,512,768]{3,2,1,0:T(8,128)(2,1)}, f32[2,512,768]{2,1,0:T(8,128)}) custom-call(s32[4]{0:T(128)} %pad_add_fusion.1.order_ref, bf16[2,512,768]{2,1,0:T(8,128)(2,1)} %copy-done.3, bf16[4,768,768]{2,1,0:T(8,128)(2,1)} %bitcast.115, f32[4,1,768]{2,1,0:T(1,128)} %reshape.404.bias_ref), custom_call_target="tpu_custom_call" | custom-call | flops 1 | bytes 1 | tf_op jit(solution)/shard_map/pallas_call | solution.py:267
  186.5 32.7 %shard_map.394 = (bf16[2,512,768]{2,1,0:T(8,128)(2,1)}, bf16[2,512,768]{2,1,0:T(8,128)(2,1)}, bf16[2,2,512,768]{3,2,1,0:T(8,128)(2,1)}, f32[4,2,512,768]{3,2,1,0...) custom-call(s32[4]{0:T(128)} %pad_add_fusion.1.order_ref, ...), custom_call_target="tpu_custom_call" | custom-call | flops 1 | bytes 1 | tf_op jit(solution)/shard_map/pallas_call | solution.py:267
  219.9 30.0 %shard_map.396 = (bf16[2,512,768]{2,1,0:T(8,128)(2,1)}, bf16[2,512,768]{2,1,0:T(8,128)(2,1)}, bf16[2,2,512,768]{3,2,1,0:T(8,128)(2,1)}, f32[4,2,8,768]{3,2,1,0:T...) custom-call(s32[4]{0:T(128)} %pad_add_fusion.1.order_ref, ...), custom_call_target="tpu_custom_call" | custom-call | flops 1 | bytes 1 | tf_op jit(solution)/shard_map/pallas_call | solution.py:267
  253.9 15.8 %shard_map.395 = (bf16[8,4,96,384]{3,2,1,0:T(8,128)(2,1)}, bf16[8,4,96,384]{3,2,1,0:T(8,128)(2,1)}, bf16[8,4,96,384]{3,2,1,0:T(8,128)(2,1)}, bf16[8,4,96,384]{3,2,1,0:T(8,128)(2,1)}) custom-call(s32[5]{0:T(128)} %pad_add_fusion.place_ref, bf16[2,512,768]{2,1,0:T(8,128)(2,1)} %get-tuple-element.383.refs_0_.grad_low_ref, bf16[2,512,768]{2,1,0:T(8,128)(2,1)} %copy-done.37, ...), custom_call_target="tpu_custom_call" | custom-call | flops 1 | bytes 1 | tf_op jit(solution)/shard_map/pallas_call | solution.py:358
  271.8 15.6 %shard_map.397 = (bf16[8,4,96,384]{3,2,1,0:T(8,128)(2,1)}, bf16[8,4,96,384]{3,2,1,0:T(8,128)(2,1)}, bf16[8,4,96,384]{3,2,1,0:T(8,128)(2,1)}, bf16[8,4,96,384]{3,2,1,0:T(8,128)(2,1)}) custom-call(s32[5]{0:T(128)} %pad_add_fusion.place_ref, bf16[2,512,768]{2,1,0:T(8,128)(2,1)} %get-tuple-element.393.refs_0_, ...), custom_call_target="tpu_custom_call" | custom-call | flops 1 | bytes 1 | tf_op jit(solution)/shard_map/pallas_call | solution.py:358
  290.2 48.7 %shard_map.398 = (bf16[2,512,768]{2,1,0:T(8,128)(2,1)}, bf16[2,512,768]{2,1,0:T(8,128)(2,1)}, bf16[2,2,512,768]{3,2,1,0:T(8,128)(2,1)}, f32[4,2,8,768]{3,2,1,0:T...) custom-call(s32[4]{0:T(128)} %pad_add_fusion.1.order_ref, ...), custom_call_target="tpu_custom_call" | custom-call | flops 1 | bytes 1 | tf_op jit(solution)/shard_map/pallas_call | solution.py:267
  340.1 4.5 shard_map.399
  349.8 24.0 %collective-permute-done.9.came_ref.came_far_ref = bf16[8,4,96,384]{3,2,1,0:T(8,128)(2,1)} collective-permute-done((bf16[8,4,96,384]{3,2,1,0:T(8,128)(2,1)}, bf16[8,4,96,384]{3,2,1,0:T(8,128)(2,1)}, u32[]{:S(2)}, u32[]{:S(2)}) %collective-permute-start.9) | collective-permute-done | bytes 2359328 | tf_op jit(solution)/shard_map/ppermute | solution.py:530
  374.2 4.6 shard_map.401
  378.7 18.1 %shard_map.402 = (bf16[8,4,96,384]{3,2,1,0:T(8,128)(2,1)}, bf16[8,4,96,384]{3,2,1,0:T(8,128)(2,1)}, bf16[8,4,96,384]{3,2,1,0:T(8,128)(2,1)}, bf16[8,4,96,384]{3,2,1,0:T(8,128)(2,1)}) custom-call(s32[5]{0:T(128)} %pad_add_fusion.place_ref, bf16[2,512,768]{2,1,0:T(8,128)(2,1)} %copy-done.3, bf16[2,512,768]{2,1,0:T(8,128)(2,1)} %copy-done.35, ...), custom_call_target="tpu_custom_call" | custom-call | flops 1 | bytes 1 | tf_op jit(solution)/shard_map/pallas_call | solution.py:358
  402.3 4.6 shard_map.403
  425.2 27.5 %collective-permute-done.16.came_ref.came_far_ref = bf16[4,4,96,384]{3,2,1,0:T(8,128)(2,1)S(1)} collective-permute-done((bf16[4,4,96,384]{3,2,1,0:T(8,128)(2,1)}, bf16[4,4,96,384]{3,2,1,0:T(8,128)(2,1)S(1)}, u32[]{:S(2)}, u32[]{:S(2)}) %collective-permute-start.16) | collective-permute-done | bytes 1179680 | tf_op jit(solution)/shard_map/ppermute | solution.py:530
  456.7 6.2 collective-permute-done.17.came_ref.came_far_ref
  466.1 9.1 %collective-permute-done.18.came_ref.came_far_ref = bf16[2,4,96,384]{3,2,1,0:T(8,128)(2,1)S(1)} collective-permute-done((bf16[2,4,96,384]{3,2,1,0:T(8,128)(2,1)}, bf16[2,4,96,384]{3,2,1,0:T(8,128)(2,1)S(1)}, u32[]{:S(2)}, u32[]{:S(2)}) %collective-permute-start.18) | collective-permute-done | bytes 589856 | tf_op jit(solution)/shard_map/ppermute | solution.py:530
  481.2 6.5 shard_map.409
  493.6 4.6 shard_map.410
  500.1 4.6 shard_map.411
  515.9 31.0 %collective-permute-done.22.came_ref.came_far_ref = bf16[2,4,96,384]{3,2,1,0:T(8,128)(2,1)S(1)} collective-permute-done((bf16[2,4,96,384]{3,2,1,0:T(8,128)(2,1)}, bf16[2,4,96,384]{3,2,1,0:T(8,128)(2,1)S(1)}, u32[]{:S(2)}, u32[]{:S(2)}) %collective-permute-start.22) | collective-permute-done | bytes 589856 | tf_op jit(solution)/shard_map/ppermute | solution.py:530
  558.9 7.7 %collective-permute-done.28.came_ref = f32[4,136,96]{2,1,0:T(8,128)S(1)} collective-permute-done((f32[4,136,96]{2,1,0:T(8,128)S(1)}, f32[4,136,96]{2,1,0:T(8,128)S(1)}, u32[]{:S(2)}, u32[]{:S(2)}) %collective-permute-start.28) | collective-permute-done | bytes 208928 | tf_op jit(solution)/shard_map/ppermute | solution.py:530
  576.4 7.8 %shard_map.420 = f32[1920,384]{1,0:T(8,128)} custom-call(s32[1,2560]{1,0:T(1,128)S(1)} %reshape_reshape.15.right_ref, bf16[2560,192]{1,0:T(8,128)(2,1)S(1)} %bitcast.106), custom_call_target="tpu_custom_call" | custom-call | flops 1 | bytes 1 | tf_op jit(solution)/shard_map/pallas_call | solution.py:499
  584.2 12.5 %collective-permute-done.32.came_ref = f32[2,136,96]{2,1,0:T(8,128)S(1)} collective-permute-done((f32[2,136,96]{2,1,0:T(8,128)}, f32[2,136,96]{2,1,0:T(8,128)S(1)}, u32[]{:S(2)}, u32[]{:S(2)}) %collective-permute-start.32) | collective-permute-done | bytes 104480 | tf_op jit(solution)/shard_map/ppermute | solution.py:530
  614.6 10.5 %collective-permute-done.34.came0_ref = bf16[1,4,96,384]{3,2,1,0:T(8,128)(2,1)S(1)} collective-permute-done((bf16[1,4,96,384]{3,2,1,0:T(8,128)(2,1)S(1)}, bf16[1,4,96,384]{3,2,1,0:T(8,128)(2,1)S(1)}, u32[]{:S(2)}, u32[]{:S(2)}) %collective-permute-start.34) | collective-permute-done | bytes 294944 | tf_op jit(solution)/shard_map/ppermute | solution.py:530
  628.6 9.0 %collective-permute-done.33.came1_ref = bf16[1,4,96,384]{3,2,1,0:T(8,128)(2,1)S(1)} collective-permute-done((bf16[1,4,96,384]{3,2,1,0:T(8,128)(2,1)}, bf16[1,4,96,384]{3,2,1,0:T(8,128)(2,1)S(1)}, u32[]{:S(2)}, u32[]{:S(2)}) %collective-permute-start.33) | collective-permute-done | bytes 294944 | tf_op jit(solution)/shard_map/ppermute | solution.py:530
  660.3 16.5 %shard_map.431 = (f32[1920,384]{1,0:T(8,128)}, f32[1920,384]{1,0:T(8,128)}, f32[1920,384]{1,0:T(8,128)}, f32[1920,384]{1,0:T(8,128)}, f32[514,96]{1,0:T(8,128)},...) custom-call(s32[1,4]{1,0:T(1,128)} %bitcast.131, ...), custom_call_target="tpu_custom_call" | custom-call | tf_op jit(solution)/shard_map/pallas_call | solution.py:882
  (327 shorter events, 198.3 us)
Async XLA Ops:
  7.3 151.8 %all-gather.3.cloned.1.call-start = ((), (), s32[]{:S(2)}) async-start(), calls=%async_computation.10 | async-start | bytes 4866048 | tf_op jit(solution)/shard_map/all_gather | solution.py:965
  9.3 177.2 %all-gather.5.cloned.1.call-start = ((), (), s32[]{:S(2)}) async-start(), calls=%async_computation.11 | async-start | bytes 9732096 | tf_op jit(solution)/shard_map/all_gather | solution.py:965
  12.0 37.7 %all-to-all-start.4 = ((bf16[8,533,96]{1,2,0:T(8,128)(2,1)}), bf16[8,533,96]{1,2,0:T(8,128)(2,1)}, u32[]{:S(2)}, u32[]{:S(2)}) async-start(bf16[8,533,96]{1,2,0:T(8,128)(2,1)} %broadcast_in_dim.22), calls=%async_computation.4 | async-start | bytes 1966080 | tf_op jit(solution)/shard_map/all_to_all | solution.py:945
  73.4 38.1 %all-to-all-start.6 = ((bf16[8,320,192]{1,2,0:T(8,128)(2,1)}), bf16[8,320,192]{1,2,0:T(8,128)(2,1)}, u32[]{:S(2)}, u32[]{:S(2)}) async-start(bf16[8,320,192]{1,2,0:T(8,128)(2,1)} %copy.172), calls=%async_computation.6 | async-start | bytes 2359296 | tf_op jit(solution)/shard_map/all_to_all | solution.py:949
  219.3 33.4 %collective-permute-start.1 = (bf16[2,512,768]{2,1,0:T(8,128)(2,1)}, bf16[2,512,768]{2,1,0:T(8,128)(2,1)S(1)}, u32[]{:S(2)}, u32[]{:S(2)}) collective-permute-start(bf16[2,512,768]{2,1,0:T(8,128)(2,1)} %get-tuple-element.385), channel_id=1, source_target_pairs={{0,1},{1,0},{2,3},{3,2},{4,5},{5,4},{6,7},{7,6},{8,9},{9,8},{10,11... | collective-permute-start | bytes 4718600 | tf_op jit(solution)/shard_map/ppermute | solution.py:530
  269.6 69.4 %collective-permute-start.6 = (bf16[8,4,96,384]{3,2,1,0:T(8,128)(2,1)}, bf16[8,4,96,384]{3,2,1,0:T(8,128)(2,1)}, u32[]{:S(2)}, u32[]{:S(2)}) collective-permute-start(bf16[8,4,96,384]{3,2,1,0:T(8,128)(2,1)} %get-tuple-element.395), channel_id=1, source_target_pairs={{0,2},{1,3},{2,0},{3,1},{4,6},{5,7},{6,4},{7,5},{8,10},{9,11},{10,... | collective-permute-start | bytes 7077896 | tf_op jit(solution)/shard_map/ppermute | solution.py:530
  270.0 69.5 %collective-permute-start.7 = (bf16[8,4,96,384]{3,2,1,0:T(8,128)(2,1)}, bf16[8,4,96,384]{3,2,1,0:T(8,128)(2,1)}, u32[]{:S(2)}, u32[]{:S(2)}) collective-permute-start(bf16[8,4,96,384]{3,2,1,0:T(8,128)(2,1)} %get-tuple-element.396), channel_id=1, source_target_pairs={{0,4},{4,0},{8,12},{12,8},{16,20},{20,16},{24,28},{28,24},{1,5},{5... | collective-permute-start | bytes 7077896 | tf_op jit(solution)/shard_map/ppermute | solution.py:530
  271.8 67.2 %collective-permute-start.10 = (bf16[2,512,768]{2,1,0:T(8,128)(2,1)S(1)}, bf16[2,512,768]{2,1,0:T(8,128)(2,1)S(1)}, u32[]{:S(2)}, u32[]{:S(2)}) collective-permute-start(bf16[2,512,768]{2,1,0:T(8,128)(2,1)S(1)} %copy-done.4), channel_id=1, source_target_pairs={{0,1},{1,0},{2,3},{3,2},{4,5},{5,4},{6,7},{7,6},{8,9},{9,8},{10,11... | collective-permute-start | bytes 4718600 | tf_op jit(solution)/shard_map/ppermute | solution.py:530
  287.4 57.3 %collective-permute-start.8 = (bf16[8,4,96,384]{3,2,1,0:T(8,128)(2,1)}, bf16[8,4,96,384]{3,2,1,0:T(8,128)(2,1)}, u32[]{:S(2)}, u32[]{:S(2)}) collective-permute-start(bf16[8,4,96,384]{3,2,1,0:T(8,128)(2,1)} %get-tuple-element.403), channel_id=1, source_target_pairs={{0,8},{4,12},{8,0},{12,4},{16,24},{20,28},{24,16},{28,20},{1,9},{5... | collective-permute-start | bytes 7077896 | tf_op jit(solution)/shard_map/ppermute | solution.py:530
  288.9 84.9 %collective-permute-start.9 = (bf16[8,4,96,384]{3,2,1,0:T(8,128)(2,1)}, bf16[8,4,96,384]{3,2,1,0:T(8,128)(2,1)}, u32[]{:S(2)}, u32[]{:S(2)}) collective-permute-start(bf16[8,4,96,384]{3,2,1,0:T(8,128)(2,1)} %get-tuple-element.401), channel_id=1, source_target_pairs={{0,2},{1,3},{2,0},{3,1},{4,6},{5,7},{6,4},{7,5},{8,10},{9,11},{10,... | collective-permute-start | bytes 7077896 | tf_op jit(solution)/shard_map/ppermute | solution.py:530
  339.0 39.7 %collective-permute-start.11 = (bf16[2,512,768]{2,1,0:T(8,128)(2,1)}, bf16[2,512,768]{2,1,0:T(8,128)(2,1)}, u32[]{:S(2)}, u32[]{:S(2)}) collective-permute-start(bf16[2,512,768]{2,1,0:T(8,128)(2,1)} %get-tuple-element.421), channel_id=1, source_target_pairs={{0,1},{1,0},{2,3},{3,2},{4,5},{5,4},{6,7},{7,6},{8,9},{9,8},{10,11... | collective-permute-start | bytes 4718600 | tf_op jit(solution)/shard_map/ppermute | solution.py:530
  339.1 39.7 %collective-permute-start.12 = (bf16[2,512,768]{2,1,0:T(8,128)(2,1)}, bf16[2,512,768]{2,1,0:T(8,128)(2,1)}, u32[]{:S(2)}, u32[]{:S(2)}) collective-permute-start(bf16[2,512,768]{2,1,0:T(8,128)(2,1)} %get-tuple-element.422), channel_id=1, source_target_pairs={{0,1},{1,0},{2,3},{3,2},{4,5},{5,4},{6,7},{7,6},{8,9},{9,8},{10,11... | collective-permute-start | bytes 4718600 | tf_op jit(solution)/shard_map/ppermute | solution.py:530
  339.6 39.2 %collective-permute-start.13 = (bf16[2,512,768]{2,1,0:T(8,128)(2,1)S(1)}, bf16[2,512,768]{2,1,0:T(8,128)(2,1)}, u32[]{:S(2)}, u32[]{:S(2)}) collective-permute-start(bf16[2,512,768]{2,1,0:T(8,128)(2,1)S(1)} %copy-done.25), channel_id=1, source_target_pairs={{0,1},{1,0},{2,3},{3,2},{4,5},{5,4},{6,7},{7,6},{8,9},{9,8},{10,11... | collective-permute-start | bytes 4718600 | tf_op jit(solution)/shard_map/ppermute | solution.py:530
  344.7 62.2 %collective-permute-start.14 = (bf16[4,4,96,384]{3,2,1,0:T(8,128)(2,1)}, bf16[4,4,96,384]{3,2,1,0:T(8,128)(2,1)S(1)}, u32[]{:S(2)}, u32[]{:S(2)}) collective-permute-start(bf16[4,4,96,384]{3,2,1,0:T(8,128)(2,1)} %get-tuple-element.430), channel_id=1, source_target_pairs={{0,4},{4,0},{8,12},{12,8},{16,20},{20,16},{24,28},{28,24},{1,5},{5... | collective-permute-start | bytes 3538952 | tf_op jit(solution)/shard_map/ppermute | solution.py:530
  373.8 37.3 %collective-permute-start.15 = (bf16[4,4,96,384]{3,2,1,0:T(8,128)(2,1)}, bf16[4,4,96,384]{3,2,1,0:T(8,128)(2,1)}, u32[]{:S(2)}, u32[]{:S(2)}) collective-permute-start(bf16[4,4,96,384]{3,2,1,0:T(8,128)(2,1)} %get-tuple-element.434), channel_id=1, source_target_pairs={{0,2},{1,3},{2,0},{3,1},{4,6},{5,7},{6,4},{7,5},{8,10},{9,11},{10,... | collective-permute-start | bytes 3538952 | tf_op jit(solution)/shard_map/ppermute | solution.py:530
  396.8 96.8 %collective-permute-start.19 = (bf16[8,4,96,384]{3,2,1,0:T(8,128)(2,1)}, bf16[8,4,96,384]{3,2,1,0:T(8,128)(2,1)}, u32[]{:S(2)}, u32[]{:S(2)}) collective-permute-start(bf16[8,4,96,384]{3,2,1,0:T(8,128)(2,1)} %get-tuple-element.463), channel_id=1, source_target_pairs={{0,2},{1,3},{2,0},{3,1},{4,6},{5,7},{6,4},{7,5},{8,10},{9,11},{10,... | collective-permute-start | bytes 7077896 | tf_op jit(solution)/shard_map/ppermute | solution.py:530
  398.4 101.7 %collective-permute-start.20 = (bf16[8,4,96,384]{3,2,1,0:T(8,128)(2,1)}, bf16[8,4,96,384]{3,2,1,0:T(8,128)(2,1)}, u32[]{:S(2)}, u32[]{:S(2)}) collective-permute-start(bf16[8,4,96,384]{3,2,1,0:T(8,128)(2,1)} %get-tuple-element.467), channel_id=1, source_target_pairs={{0,4},{4,0},{8,12},{12,8},{16,20},{20,16},{24,28},{28,24},{1,5},{5... | collective-permute-start | bytes 7077896 | tf_op jit(solution)/shard_map/ppermute | solution.py:530
  399.9 52.8 %collective-permute-start.16 = (bf16[4,4,96,384]{3,2,1,0:T(8,128)(2,1)}, bf16[4,4,96,384]{3,2,1,0:T(8,128)(2,1)S(1)}, u32[]{:S(2)}, u32[]{:S(2)}) collective-permute-start(bf16[4,4,96,384]{3,2,1,0:T(8,128)(2,1)} %get-tuple-element.440), channel_id=1, source_target_pairs={{0,16},{4,20},{8,24},{12,28},{16,0},{20,4},{24,8},{28,12},{1,17},{... | collective-permute-start | bytes 3538952 | tf_op jit(solution)/shard_map/ppermute | solution.py:530
  417.9 60.5 %all-to-all-start.8 = ((bf16[4,1024,192]{1,2,0:T(8,128)(2,1)}), bf16[4,1024,192]{1,2,0:T(8,128)(2,1)}, u32[]{:S(2)}, u32[]{:S(2)}) async-start(bf16[4,1024,192]{1,2,0:T(8,128)(2,1)} %copy.188), calls=%async_computation.8 | async-start | bytes 3145728 | tf_op jit(solution)/shard_map/all_to_all | solution.py:1113
  422.4 40.5 %collective-permute-start.17 = (bf16[2,4,96,384]{3,2,1,0:T(8,128)(2,1)}, bf16[2,4,96,384]{3,2,1,0:T(8,128)(2,1)S(1)}, u32[]{:S(2)}, u32[]{:S(2)}) collective-permute-start(bf16[2,4,96,384]{3,2,1,0:T(8,128)(2,1)} %get-tuple-element.444), channel_id=1, source_target_pairs={{0,8},{4,12},{8,0},{12,4},{16,24},{20,28},{24,16},{28,20},{1,9},{5... | collective-permute-start | bytes 1769480 | tf_op jit(solution)/shard_map/ppermute | solution.py:530
  423.9 51.2 %collective-permute-start.18 = (bf16[2,4,96,384]{3,2,1,0:T(8,128)(2,1)}, bf16[2,4,96,384]{3,2,1,0:T(8,128)(2,1)S(1)}, u32[]{:S(2)}, u32[]{:S(2)}) collective-permute-start(bf16[2,4,96,384]{3,2,1,0:T(8,128)(2,1)} %get-tuple-element.448), channel_id=1, source_target_pairs={{0,8},{4,12},{8,0},{12,4},{16,24},{20,28},{24,16},{28,20},{1,9},{5... | collective-permute-start | bytes 1769480 | tf_op jit(solution)/shard_map/ppermute | solution.py:530
  452.7 58.7 %collective-permute-start.21 = (bf16[4,4,96,384]{3,2,1,0:T(8,128)(2,1)}, bf16[4,4,96,384]{3,2,1,0:T(8,128)(2,1)}, u32[]{:S(2)}, u32[]{:S(2)}) collective-permute-start(bf16[4,4,96,384]{3,2,1,0:T(8,128)(2,1)} %get-tuple-element.479), channel_id=1, source_target_pairs={{0,4},{4,0},{8,12},{12,8},{16,20},{20,16},{24,28},{28,24},{1,5},{5... | collective-permute-start | bytes 3538952 | tf_op jit(solution)/shard_map/ppermute | solution.py:530
  489.2 85.5 %all-to-all-start.9 = ((bf16[8,320,192]{1,2,0:T(8,128)(2,1)}), bf16[8,320,192]{1,2,0:T(8,128)(2,1)}, u32[]{:S(2)}, u32[]{:S(2)}) async-start(bf16[8,320,192]{1,2,0:T(8,128)(2,1)} %copy.190), calls=%async_computation.9 | async-start | bytes 2359296 | tf_op jit(solution)/shard_map/all_to_all | solution.py:949
  498.2 52.0 %collective-permute-start.24 = (bf16[4,4,96,384]{3,2,1,0:T(8,128)(2,1)}, bf16[4,4,96,384]{3,2,1,0:T(8,128)(2,1)}, u32[]{:S(2)}, u32[]{:S(2)}) collective-permute-start(bf16[4,4,96,384]{3,2,1,0:T(8,128)(2,1)} %get-tuple-element.491), channel_id=1, source_target_pairs={{0,4},{4,0},{8,12},{12,8},{16,20},{20,16},{24,28},{28,24},{1,5},{5... | collective-permute-start | bytes 3538952 | tf_op jit(solution)/shard_map/ppermute | solution.py:530
  504.7 49.6 %collective-permute-start.25 = (bf16[4,4,96,384]{3,2,1,0:T(8,128)(2,1)}, bf16[4,4,96,384]{3,2,1,0:T(8,128)(2,1)}, u32[]{:S(2)}, u32[]{:S(2)}) collective-permute-start(bf16[4,4,96,384]{3,2,1,0:T(8,128)(2,1)} %get-tuple-element.495), channel_id=1, source_target_pairs={{0,2},{1,3},{2,0},{3,1},{4,6},{5,7},{6,4},{7,5},{8,10},{9,11},{10,... | collective-permute-start | bytes 3538952 | tf_op jit(solution)/shard_map/ppermute | solution.py:530
  508.3 38.6 %collective-permute-start.22 = (bf16[2,4,96,384]{3,2,1,0:T(8,128)(2,1)}, bf16[2,4,96,384]{3,2,1,0:T(8,128)(2,1)S(1)}, u32[]{:S(2)}, u32[]{:S(2)}) collective-permute-start(bf16[2,4,96,384]{3,2,1,0:T(8,128)(2,1)} %get-tuple-element.483), channel_id=1, source_target_pairs={{0,4},{4,0},{8,12},{12,8},{16,20},{20,16},{24,28},{28,24},{1,5},{5... | collective-permute-start | bytes 1769480 | tf_op jit(solution)/shard_map/ppermute | solution.py:530
  511.0 47.1 %collective-permute-start.26 = (f32[136,768]{1,0:T(8,128)S(1)}, f32[136,768]{1,0:T(8,128)S(1)}, u32[]{:S(2)}, u32[]{:S(2)}) collective-permute-start(f32[136,768]{1,0:T(8,128)S(1)} %get-tuple-element.498), channel_id=1, source_target_pairs={{0,2},{1,3},{2,0},{3,1},{4,6},{5,7},{6,4},{7,5},{8,10},{9,11},{10,... | collective-permute-start | bytes 1253384 | tf_op jit(solution)/shard_map/ppermute | solution.py:530
  514.4 57.1 %collective-permute-start.27 = (bf16[2,4,96,384]{3,2,1,0:T(8,128)(2,1)}, bf16[2,4,96,384]{3,2,1,0:T(8,128)(2,1)S(1)}, u32[]{:S(2)}, u32[]{:S(2)}) collective-permute-start(bf16[2,4,96,384]{3,2,1,0:T(8,128)(2,1)} %get-tuple-element.503), channel_id=1, source_target_pairs={{0,8},{4,12},{8,0},{12,4},{16,24},{20,28},{24,16},{28,20},{1,9},{5... | collective-permute-start | bytes 1769480 | tf_op jit(solution)/shard_map/ppermute | solution.py:530
  553.1 45.7 %collective-permute-start.29 = (bf16[2,4,96,384]{3,2,1,0:T(8,128)(2,1)}, bf16[2,4,96,384]{3,2,1,0:T(8,128)(2,1)}, u32[]{:S(2)}, u32[]{:S(2)}) collective-permute-start(bf16[2,4,96,384]{3,2,1,0:T(8,128)(2,1)} %get-tuple-element.514), channel_id=1, source_target_pairs={{0,8},{4,12},{8,0},{12,4},{16,24},{20,28},{24,16},{28,20},{1,9},{5... | collective-permute-start | bytes 1769480 | tf_op jit(solution)/shard_map/ppermute | solution.py:530
  557.2 45.5 %collective-permute-start.31 = (bf16[2,4,96,384]{3,2,1,0:T(8,128)(2,1)}, bf16[2,4,96,384]{3,2,1,0:T(8,128)(2,1)}, u32[]{:S(2)}, u32[]{:S(2)}) collective-permute-start(bf16[2,4,96,384]{3,2,1,0:T(8,128)(2,1)} %get-tuple-element.520), channel_id=1, source_target_pairs={{0,8},{4,12},{8,0},{12,4},{16,24},{20,28},{24,16},{28,20},{1,9},{5... | collective-permute-start | bytes 1769480 | tf_op jit(solution)/shard_map/ppermute | solution.py:530
  568.2 39.6 %collective-permute-start.37 = (bf16[1,4,96,384]{3,2,1,0:T(8,128)(2,1)}, bf16[1,4,96,384]{3,2,1,0:T(8,128)(2,1)S(1)}, u32[]{:S(2)}, u32[]{:S(2)}) collective-permute-start(bf16[1,4,96,384]{3,2,1,0:T(8,128)(2,1)} %get-tuple-element.535), channel_id=1, source_target_pairs={{0,16},{4,20},{8,24},{12,28},{16,0},{20,4},{24,8},{28,12},{1,17},{... | collective-permute-start | bytes 884744 | tf_op jit(solution)/shard_map/ppermute | solution.py:530
  571.5 36.3 %collective-permute-start.36 = (bf16[1,4,96,384]{3,2,1,0:T(8,128)(2,1)}, bf16[1,4,96,384]{3,2,1,0:T(8,128)(2,1)S(1)}, u32[]{:S(2)}, u32[]{:S(2)}) collective-permute-start(bf16[1,4,96,384]{3,2,1,0:T(8,128)(2,1)} %get-tuple-element.533), channel_id=1, source_target_pairs={{0,16},{4,20},{8,24},{12,28},{16,0},{20,4},{24,8},{28,12},{1,17},{... | collective-permute-start | bytes 884744 | tf_op jit(solution)/shard_map/ppermute | solution.py:530
  (74 other events, 996.3 us)
Sparse Core Ops, SparseCore 0:
  11.6 74.9 all-gather.2
  90.1 91.2 all-gather.4
